TPU v7x, 32 devices: a whole 2x2x4 slice. The times are simulated.
32 devices in a mesh: slab: 4 (over y, x), brick: 8 (over z, core).
Axes of the slice: x: 2, y: 2, z: 4, core: 2. Of those that a mesh axis runs over, the one named last changes fastest.
Arguments:
- verts: float32 [32768, 3, 128], P(('slab', 'brick')), may hold values from -4.2 to 4.2
- stiffness: float32 [32768, 128], P(('slab', 'brick')), may hold values from 0.2 to 2
- local_pairs: int32 [32, 2, 256], P(('slab', 'brick')), may hold values from 0 to 1023, as said below
- border_pick: int32 [32, 128], P(('slab', 'brick')), may hold values from 0 to 1023
- recv_src: int32 [32, 8, 8], P(('slab', 'brick')), may hold values from 0 to 127
- recv_pair: int32 [32, 8, 8], P(('slab', 'brick')), may hold values from -1 to 1023, as said below
- face_pick: int32 [32, 2, 64], P(('slab', 'brick')), may hold values from 0 to 1023
- face_pair: int32 [32, 2, 64], P(('slab', 'brick')), may hold values from -1 to 1023, as said below
Outputs:
- membrane_force: float32 [32768, 3, 128], P(('slab', 'brick'))
Inputs may be any that keep to these rules, and one draw needn't show every extreme that they name: `local_pairs`: the two rows of a pair name different patches. `recv_pair`: -1 marks an empty slot; the slots for a device's own brick are empty. `face_pair`: -1 marks an empty slot.
All inputs are finite; a program needn't handle non-finite values.
Results may differ from a plain program's by a relative error of at most 0.0001.
Values sent between devices are 32-bit elements; how exact they have to be, the bound alone decides.
No kernel may reach another device: no remote copies, remote signals or barrier semaphores. Data moves between devices by JAX's collectives and lax.ppermute only.
A program may use at most 128 MiB of HBM per device.

v0:
```python
import math

import jax
import jax.numpy as jnp
from jax import lax
from jax.sharding import PartitionSpec as P

highest = lax.Precision.HIGHEST


def with_halo(cells, sides, width):
    for axis, dim in sides:
        count = lax.axis_size(axis)
        ends = count - 1
        head = lax.slice_in_dim(cells, 0, width, axis=dim)
        tail = lax.slice_in_dim(cells, cells.shape[dim] - width, cells.shape[dim], axis=dim)
        cells = jnp.concatenate(
            [
                lax.ppermute(tail, axis, [(i, (i + 1) % count) for i in range(ends)]),
                cells,
                lax.ppermute(head, axis, [((i + 1) % count, i) for i in range(ends)]),
            ],
            axis=dim,
        )
    return cells


def centroids(points):
    return (points + jnp.roll(points, -1, axis=-1) + jnp.roll(points, -2, axis=-1)) / 3.0


def tile_forces(own_points, far_centres, far_weight):
    own_sq = jnp.sum(own_points * own_points, axis=1)
    far_sq = jnp.sum(far_centres * far_centres, axis=1)
    cross_dot = jnp.einsum("pci,pcj->pij", own_points, far_centres, precision=highest)
    dist_sq = own_sq[:, :, None] + far_sq[:, None, :] - 2.0 * cross_dot
    energy = far_weight[:, None, :] * jnp.exp(-0.5 * dist_sq) / own_points.shape[-1]
    row_total = jnp.sum(energy, axis=2)
    col_total = jnp.sum(energy, axis=1)
    pushed = own_points * row_total[:, None, :] - jnp.einsum(
        "pcj,pij->pci", far_centres, energy, precision=highest
    )
    reaction = far_centres * col_total[:, None, :] - jnp.einsum(
        "pci,pij->pcj", own_points, energy, precision=highest
    )
    return (pushed, reaction)


def blocked(func, arrays):
    count = arrays[0].shape[0]
    step_rows = math.gcd(count, 16)
    shaped = tuple(
        (array.reshape((count // step_rows, step_rows) + array.shape[1:]) for array in arrays)
    )
    results = lax.map(func, shaped)
    return tuple((result.reshape((count,) + result.shape[2:]) for result in results))


def body(verts, stiffness, local_pairs, border_pick, recv_src, recv_pair, face_pick, face_pair):
    vert_count = verts.shape[-1]
    centres = centroids(verts)

    def pack_rows(rows):
        return jnp.concatenate([verts[rows], stiffness[rows][..., None, :]], axis=-2)

    def remote(packed, targets, allowed, pushed):
        usable = (targets >= 0) & allowed
        clipped = jnp.maximum(targets, 0)

        def far_tiles(pieces):
            target_idx, packed_rows, usable_rows = pieces
            weight = packed_rows[:, 3] * usable_rows.astype(jnp.float32)[:, None]
            return tile_forces(verts[target_idx], centroids(packed_rows[:, :3]), weight)

        push_far, react_far = blocked(far_tiles, (clipped, packed, usable))
        return (pushed.at[clipped].add(push_far), react_far)

    target_loc = local_pairs[0, 0]
    anchor_loc = local_pairs[0, 1]

    def local_tiles(pieces):
        target_idx, anchor_idx = pieces
        return tile_forces(verts[target_idx], centres[anchor_idx], stiffness[anchor_idx])

    push_loc, react_loc = blocked(local_tiles, (target_loc, anchor_loc))
    pushed = jnp.zeros_like(verts).at[target_loc].add(push_loc)
    reaction = jnp.zeros_like(verts).at[anchor_loc].add(react_loc)
    brick_pushed = pushed
    brick_reaction = reaction
    bricks = lax.axis_size("brick")
    border_count = border_pick.shape[1]
    every = lax.all_gather(pack_rows(border_pick[0]), "brick", axis=0, tiled=True)
    flat = (jnp.arange(bricks, dtype=jnp.int32)[:, None] * border_count + recv_src[0]).reshape(-1)
    brick_pushed, react_far = remote(every[flat], recv_pair[0].reshape(-1), True, brick_pushed)
    partial_sums = (
        jnp.zeros((bricks * border_count, 3, vert_count), jnp.float32).at[flat].add(react_far)
    )
    mine = lax.psum_scatter(partial_sums, "brick", scatter_dimension=0, tiled=True)
    brick_reaction = brick_reaction.at[border_pick[0]].add(mine)
    pushed = brick_pushed
    face_pushed = pushed
    face_reaction = brick_reaction
    facing = face_pick.shape[2]
    rows = face_pick[0].reshape(-1)
    extended = with_halo(pack_rows(rows), (("slab", 0),), facing)
    incoming = jnp.concatenate([extended[:facing], extended[3 * facing :]], axis=0)
    layer = lax.axis_index("slab")
    layers = lax.axis_size("slab")
    allowed = jnp.concatenate(
        [jnp.full((facing,), layer > 0), jnp.full((facing,), layer < layers - 1)]
    )
    face_pushed, react_far = remote(incoming, face_pair[0].reshape(-1), allowed, face_pushed)
    returned = with_halo(react_far, (("slab", 0),), facing)
    face_reaction = face_reaction.at[rows[:facing]].add(returned[:facing])
    face_reaction = face_reaction.at[rows[facing:]].add(returned[3 * facing :])
    pushed = face_pushed
    return (
        pushed
        + (
            face_reaction
            + jnp.roll(face_reaction, 1, axis=-1)
            + jnp.roll(face_reaction, 2, axis=-1)
        )
        / 3.0
    )


def solution(mesh):
    placed = (
        P(("slab", "brick"), None, None),
        P(("slab", "brick"), None),
        P(("slab", "brick"), None, None),
        P(("slab", "brick"), None),
        P(("slab", "brick"), None, None),
        P(("slab", "brick"), None, None),
        P(("slab", "brick"), None, None),
        P(("slab", "brick"), None, None),
    )
    return jax.shard_map(
        body,
        mesh=mesh,
        in_specs=placed,
        out_specs=P(("slab", "brick"), None, None),
        check_vma=False,
    )
```

profile of v0, /device:TPU:11, one launch (start us, length us, event | category | flops | bytes accessed | tf_op | source)
XLA Modules:
  0.0 391.6 jit_solution(6549210688689407000)
XLA Ops:
  13.1 3.1 collective-permute-start
  16.3 2.8 collective-permute-start.1
  19.1 2.6 copy.35
  21.6 2.5 slice.168
  24.1 2.5 slice.170
  26.8 6.2 %fusion.52 = f32[1024,3,128]{2,1,0:T(4,128)} fusion(f32[1024,3,1]{2,1,0:T(4,128)S(1)} %bitcast.197, f32[1024,3,127]{2,1,0:T(4,128)} %slice.168, f32[1024,3,2]{2,1,0:T(4,128)S(1)} %bitcast.198, f32[1024,3,126]{2,1,0:T(4,128)} %slice.170, f32[1024,3,128]{2,0,1:T(8,128)} %param.14), kind=kLoop, calls=%fused_computation.109 | loop fusion | flops 1966080 | bytes 6291456 | tf_op jit(solution)/shard_map/div | solution.py:29
  33.0 147.0 %while.36 = (s32[]{:T(128)}, f32[16,16,3,128]{3,2,1,0:T(4,128)S(1)}, f32[16,16,3,128]{3,2,1,0:T(4,128)}, s32[16,16]{1,0:T(8,128)S(1)}, f32[1024,3,128]{2,1,0:T(4...) while((s32[]{:T(128)}, ...), condition=%wide.region_5.6_spmd, body=%wide.region_0.5_spmd.sunk | while | flops 30451808 | bytes 3622053 | solution.py:55
  36.4 2.4 fusion.118
  54.8 2.4 fusion.118
  73.2 2.4 fusion.118
  91.5 2.4 fusion.118
  109.9 2.4 fusion.118
  182.4 8.3 %scatter_fusion = f32[1024,3,128]{2,1,0:T(4,128)S(1)} fusion(f32[1024,3,128]{2,1,0:T(4,128)S(1)} %broadcast.313.clone, s32[256]{0:T(256)S(1)} %bitcast.217, f32[256,3,128]{2,1,0:T(4,128)S(1)} %bitcast.210), kind=kCustom, calls=%fused_computation.10 | custom fusion | flops 98304 | bytes 1180672 | tf_op jit(solution)/shard_map/scatter-add | solution.py:87
  191.8 4.3 %copy.36 = f32[1024,4,128]{2,1,0:T(4,128)} copy(f32[1024,4,128]{2,0,1:T(8,128)} %all-gather.2.cloned.1.call-done) | data formatting | bytes 4194304 | tf_op jit(solution)/shard_map/all_gather | solution.py:92
  198.3 36.1 %while.37 = (s32[]{:T(128)}, f32[4,16,3,128]{3,2,1,0:T(4,128)}, f32[4,16,3,128]{3,2,1,0:T(4,128)}, s32[4,16]{1,0:T(4,128)S(1)}, f32[1024,3,128]{2,1,0:T(4,128)},...) while((s32[]{:T(128)}, f32[4,16,3,128]{3,2,1,0:T(4,128)}, ...), condition=%wide.region_12.13_spmd, body=%wide.region_7.0_spmd.sunk | while | flops 30497856 | bytes 3805553 | solution.py:55
  201.2 2.4 fusion.128
  210.2 2.4 fusion.128
  219.1 2.4 fusion.128
  228.1 2.4 fusion.128
  236.0 6.8 %scatter_fusion.1 = f32[1024,3,128]{2,1,0:T(4,128)} fusion(f32[1024,3,128]{2,1,0:T(4,128)} %broadcast.313.clone.1, s32[64]{0:T(128)S(1)} %fusion.57, f32[64,3,128]{2,1,0:T(4,128)S(1)} %bitcast.215), kind=kCustom, calls=%fused_computation.11 | custom fusion | flops 24576 | bytes 295168 | tf_op jit(solution)/shard_map/scatter-add | solution.py:96
  242.8 67.1 %while.38 = (s32[]{:T(128)}, f32[8,16,3,128]{3,2,1,0:T(4,128)}, f32[8,16,3,128]{3,2,1,0:T(4,128)S(1)}, s32[8,16]{1,0:T(8,128)S(1)}, f32[1024,3,128]{2,1,0:T(4,12...) while((s32[]{:T(128)}, f32[8,16,3,128]{3,2,1,0:T(4,128)}, ...), condition=%wide.region_21.22_spmd, body=%wide.region_16.21_spmd.sunk | while | flops 30497856 | bytes 3886965 | solution.py:55
  279.0 2.4 fusion.138
  304.2 2.4 fusion.138
  310.7 3.3 collective-permute-start.2
  317.0 5.2 %scatter_fusion.2 = f32[1024,3,128]{2,1,0:T(4,128)S(1)} fusion(f32[1024,3,128]{2,1,0:T(4,128)S(1)} %scatter_fusion, s32[128]{0:T(128)S(1)} %fusion.56, f32[128,3,128]{2,1,0:T(4,128)S(1)} %constant_dynamic-slice_fusion.5), kind=kCustom, calls=%fused_computation.12 | custom fusion | flops 49152 | bytes 590336 | tf_op jit(solution)/shard_map/scatter-add | solution.py:99
  322.2 2.7 scatter_fusion.3
  325.0 2.7 scatter_fusion.4
  330.0 3.4 fusion.54
  333.4 25.1 %scatter_fusion.5 = f32[1024,3,128]{2,1,0:T(4,128)} fusion(f32[1024,3,128]{2,1,0:T(4,128)} %fusion.54, s32[256]{0:T(256)S(1)} %bitcast.216, f32[256,3,128]{2,1,0:T(4,128)S(1)} %bitcast.209), kind=kCustom, calls=%fused_computation.15 | custom fusion | flops 98304 | bytes 1180672 | tf_op jit(solution)/shard_map/scatter-add | solution.py:86
  358.5 8.4 %scatter_fusion.6 = f32[1024,3,128]{2,1,0:T(4,128)} fusion(f32[1024,3,128]{2,1,0:T(4,128)} %scatter_fusion.5, s32[64]{0:T(128)S(1)} %reshape.560, f32[64,3,128]{2,1,0:T(4,128)} %bitcast.41), kind=kCustom, calls=%fused_computation.16 | custom fusion | flops 24576 | bytes 295168 | tf_op jit(solution)/shard_map/scatter-add | solution.py:76
  366.8 15.1 %scatter_fusion.7 = f32[1024,3,128]{2,1,0:T(4,128)} fusion(f32[1024,3,128]{2,1,0:T(4,128)} %scatter_fusion.6, s32[128]{0:T(128)S(1)} %reshape.568, f32[128,3,128]{2,1,0:T(4,128)} %bitcast.42), kind=kCustom, calls=%fused_computation.17 | custom fusion | flops 49152 | bytes 590336 | tf_op jit(solution)/shard_map/scatter-add | solution.py:76
  382.0 2.8 copy.40
  (412 shorter events, 241.8 us)
Async XLA Ops:
  6.5 4.4 %copy-start.1 = (f32[1024,3,128]{2,0,1:T(8,128)S(1)}, f32[1024,3,128]{2,0,1:T(8,128)}, u32[]{:S(2)}) copy-start(f32[1024,3,128]{2,0,1:T(8,128)} %param.14) | copy-start | bytes 4718596
  6.5 2.8 copy-start.2
  6.5 4.2 %copy-start.9 = (s32[1,2,64]{2,1,0:T(2,128)S(1)}, s32[1,2,64]{2,1,0:T(2,128)}, u32[]{:S(2)}) copy-start(s32[1,2,64]{2,1,0:T(2,128)} %param.20) | copy-start | bytes 1540
  6.5 185.3 %all-gather.2.cloned.1.call-start = ((), (), s32[]{:S(2)}) async-start(), calls=%async_computation | async-start | bytes 2359296 | tf_op jit(solution)/shard_map/all_gather | solution.py:92
  10.7 305.3 %all-reduce.4.cloned.1.call-start = ((), (), s32[]{:S(2)}) async-start(), calls=%async_computation.1 | async-start | bytes 4194304
  13.1 177.6 %collective-permute-start = (f32[64,4,128]{2,0,1:T(8,128)}, f32[64,4,128]{2,0,1:T(8,128)}, u32[]{:S(2)}, u32[]{:S(2)}) collective-permute-start(f32[64,4,128]{2,0,1:T(8,128)} %get-tuple-element.247), channel_id=1, source_target_pairs={{0,8},{8,16},{16,24},{1,9},{9,17},{17,25},{2,10},{10,18},{18,26},{... | collective-permute-start | bytes 393224 | tf_op jit(solution)/shard_map/ppermute | solution.py:19
  16.3 174.5 %collective-permute-start.1 = (f32[64,4,128]{2,0,1:T(8,128)}, f32[64,4,128]{2,0,1:T(8,128)}, u32[]{:S(2)}, u32[]{:S(2)}) collective-permute-start(f32[64,4,128]{2,0,1:T(8,128)} %get-tuple-element.248), channel_id=1, source_target_pairs={{8,0},{16,8},{24,16},{9,1},{17,9},{25,17},{10,2},{18,10},{26,18},{... | collective-permute-start | bytes 393224 | tf_op jit(solution)/shard_map/ppermute | solution.py:21
  24.1 2.5 copy-start.6
  32.9 147.2 %copy-start.7 = (s32[1,8,8]{2,1,0:T(8,128)S(1)}, s32[1,8,8]{2,1,0:T(8,128)}, u32[]{:S(2)}) copy-start(s32[1,8,8]{2,1,0:T(8,128)} %param.18) | copy-start | bytes 772
  32.9 147.3 %copy-start.8 = (s32[1,2,64]{2,1,0:T(2,128)S(1)}, s32[1,2,64]{2,1,0:T(2,128)}, u32[]{:S(2)}) copy-start(s32[1,2,64]{2,1,0:T(2,128)} %param.21) | copy-start | bytes 1540
  33.0 147.4 %copy-start.5 = (s32[1,8,8]{2,1,0:T(8,128)S(1)}, s32[1,8,8]{2,1,0:T(8,128)}, u32[]{:S(2)}) copy-start(s32[1,8,8]{2,1,0:T(8,128)} %param.19) | copy-start | bytes 772
  33.0 148.0 %copy-start.10 = (u32[32]{0:T(128)S(1)}, u32[32]{0:T(128)}, u32[]{:S(2)}) copy-start(u32[32]{0:T(128)} %constant.120) | copy-start | bytes 388
  180.0 2.2 copy-start
  180.0 2.4 copy-start.3
  234.4 1.6 copy-start.4
  310.7 11.5 %collective-permute-start.2 = (f32[64,3,128]{2,1,0:T(4,128)}, f32[64,3,128]{2,1,0:T(4,128)S(1)}, u32[]{:S(2)}, u32[]{:S(2)}) collective-permute-start(f32[64,3,128]{2,1,0:T(4,128)} %bitcast.34), channel_id=1, source_target_pairs={{0,8},{8,16},{16,24},{1,9},{9,17},{17,25},{2,10},{10,18},{18,26},{... | collective-permute-start | bytes 294920 | tf_op jit(solution)/shard_map/ppermute | solution.py:19
  314.0 11.0 %collective-permute-start.3 = (f32[64,3,128]{2,1,0:T(4,128)}, f32[64,3,128]{2,1,0:T(4,128)S(1)}, u32[]{:S(2)}, u32[]{:S(2)}) collective-permute-start(f32[64,3,128]{2,1,0:T(4,128)} %bitcast.37), channel_id=1, source_target_pairs={{8,0},{16,8},{24,16},{9,1},{17,9},{25,17},{10,2},{18,10},{26,18},{... | collective-permute-start | bytes 294920 | tf_op jit(solution)/shard_map/ppermute | solution.py:21
Sparse Core Ops, SparseCore 0:
  10.9 30.6 all-gather.1
  243.0 64.3 all-reduce.3
where the time goes:
time: 398 us; the launch traced here: 392 us
  matrix products  163 us (41%)
  local copies, waits for them, and re-layouts  110 us (28%)
  other arithmetic  91.2 us (23%)
  between operations  14.3 us (4%)
  starting transfers between devices  11.2 us (3%)
    dot_general x28, matrix products, tile_forces(): jnp.einsum('pci,pcj->pij', own_points, far_centres, precision=highest)  67.2 us
    dot_general x28, matrix products, tile_forces(): jnp.einsum('pcj,pij->pci', far_centres, energy, precision=highest)  56.1 us
    dot_general x28, matrix products, tile_forces(): jnp.einsum('pci,pij->pcj', own_points, energy, precision=highest)  39.9 us
    gather x16, local copies, waits for them, and re-layouts, local_tiles(): centres[anchor_idx]  34.9 us
    gather x12, local copies, waits for them, and re-layouts, far_tiles(): return tile_forces(verts[target_idx], centroids(packed_rows[:, :3]), weight)  26.2 us
    scatter-add x1, other arithmetic, body(): pushed = jnp.zeros_like(verts).at[target_loc].add(push_loc)  25.1 us
    scatter-add x2, other arithmetic, remote(): return (pushed.at[clipped].add(push_far), react_far)  23.5 us
    gather x16, local copies, waits for them, and re-layouts, local_tiles(): verts[target_idx]  9.4 us
  transfers between devices with their start and end apart: 6, of which 0 were waited for; matrix products, arithmetic and copies ran while one was open for 64% of the time, Pallas kernels for 0%

commit v1 on v0

v1 whole, which is shorter than its diff:
```python
import functools
import math

import jax
import jax.numpy as jnp
from jax import lax
from jax.experimental import pallas as pl
from jax.experimental.pallas import tpu as pltpu
from jax.sharding import PartitionSpec as P

F32 = jnp.float32
BF16 = jnp.bfloat16
ALPHA = math.sqrt(math.log2(math.e))
OFF = -1.0e5
VMEM_LIMIT = 48 * 1024 * 1024


def rows8(v=None):
    return lax.broadcasted_iota(jnp.int32, (8, 128), 0)


def split3(x):
    high = x.astype(BF16).astype(F32)
    rest = x - high
    mid = rest.astype(BF16).astype(F32)
    return high, mid, rest - mid


def own_block(entry, row):
    return jnp.where(row < 4, entry, jnp.where(row == 7, 1.0, 0.0))


def far_block(entry, row):
    return jnp.where(row < 3, pltpu.roll(entry, 4, 0), jnp.where(row == 3, 1.0, entry))


def energy_pair(owns, fars):
    us = [split3(u) for u in owns]
    ws = [split3(w) for w in fars]
    left = jnp.concatenate([part for h, m, l in us for part in (h, h, m, m, h, l)], axis=0).astype(BF16)
    blocks = [jnp.concatenate([h, m, h, m, l, h], axis=0).astype(BF16) for h, m, l in ws]
    empty = jnp.zeros_like(blocks[0])
    right = jnp.concatenate(
        [
            jnp.concatenate([blocks[0], empty], axis=1),
            jnp.concatenate([empty, blocks[1]], axis=1),
        ],
        axis=0,
    )
    exponent = lax.dot_general(left, right, (((0,), (0,)), ((), ())), preferred_element_type=F32)
    energy = jnp.exp2(exponent)
    high = energy.astype(BF16)
    low = (energy - high.astype(F32)).astype(BF16)
    return high, low, us, ws


def thin(parts):
    stack = jnp.concatenate([part for h, m, l in parts for part in (h, m)], axis=0).astype(BF16)
    return jnp.concatenate([stack, stack], axis=1)


def fold(result):
    first = result[0:8, 0:128] + result[8:16, 0:128]
    second = result[16:24, 128:256] + result[24:32, 128:256]
    return first, second


def pushes(high, low, owns, ws):
    tall = jnp.concatenate(
        [
            jnp.concatenate([high[:, 0:128], low[:, 0:128]], axis=1),
            jnp.concatenate([high[:, 128:256], low[:, 128:256]], axis=1),
        ],
        axis=0,
    )
    result = lax.dot_general(thin(ws), tall, (((1,), (1,)), ((), ())), preferred_element_type=F32)
    return [(own * total[3:4] - total) * (1.0 / ALPHA) for own, total in zip(owns, fold(result))]


def reactions(high, low, fars, us):
    tall = jnp.concatenate([high, low], axis=0)
    result = lax.dot_general(thin(us), tall, (((1,), (0,)), ((), ())), preferred_element_type=F32)
    out = []
    for far, total in zip(fars, fold(result)):
        react = (far * total[7:8] - total) * (1.0 / (3.0 * ALPHA))
        out.append(react + pltpu.roll(react, 1, 1) + pltpu.roll(react, 2, 1))
    return out


def entry_at(ref, index):
    return ref[pl.ds(pl.multiple_of(index * 8, 8), 8), :]


def pack_kernel(
    flags, recv_src, recv_pair, face_pick, face_pair, verts, stiffness,
    table, brick_msg, face_lo, face_hi, coords, sems,
):
    patches = stiffness.shape[0]
    copies = [pltpu.make_async_copy(verts.at[:, c, :], coords.at[c], sems.at[c]) for c in range(3)]
    for copy in copies:
        copy.start()
    for copy in copies:
        copy.wait()

    @pl.loop(0, patches // 8, unroll=4)
    def build(step):
        base = pl.multiple_of(step * 8, 8)
        xs = [coords[c, pl.ds(base, 8), :] * ALPHA for c in range(3)]
        cs = [(x + pltpu.roll(x, 127, 1) + pltpu.roll(x, 126, 1)) * (1.0 / 3.0) for x in xs]
        strength = stiffness[pl.ds(base, 8), :]
        own = -0.5 * (xs[0] * xs[0] + xs[1] * xs[1] + xs[2] * xs[2])
        far = jnp.log2(strength) - 7.0 - 0.5 * (cs[0] * cs[0] + cs[1] * cs[1] + cs[2] * cs[2])
        for k, value in enumerate(xs + [own] + cs + [far]):
            table[pl.ds(step * 64 + k, 8, stride=8), :] = value

    row = rows8()
    bricks, slots = recv_pair.shape[1], recv_pair.shape[2]

    @pl.loop(0, bricks)
    def brick(s):
        for k in range(slots):
            target = recv_pair[0, s, k]
            index = jnp.where(target >= 0, recv_src[0, s, k], -1).astype(F32)
            entry = entry_at(table, jnp.maximum(target, 0))
            slot = s * slots + k
            brick_msg[slot] = jnp.where(row == 3, index, entry)[0:4]

    facing = face_pick.shape[2]

    @pl.loop(0, facing, unroll=4)
    def face(k):
        for side, out in ((0, face_lo), (1, face_hi)):
            target = face_pair[0, side, k]
            usable = (target >= 0) & (flags[side] > 0)
            own = entry_at(table, jnp.maximum(target, 0))
            own = jnp.where((row == 3) & jnp.logical_not(usable), OFF, own)
            out[k] = jnp.where(row < 4, own, entry_at(table, face_pick[0, side, k]))


def local_kernel(local_pairs, table, force):
    force[...] = jnp.zeros_like(force)
    row = rows8()
    count = local_pairs.shape[2]

    @pl.loop(0, count // 4)
    def group(step):
        for half in range(2):
            first = step * 4 + half * 2
            targets = [local_pairs[0, 0, first + k] for k in range(2)]
            anchors = [local_pairs[0, 1, first + k] for k in range(2)]
            owns = [own_block(entry_at(table, t), row) for t in targets]
            fars = [far_block(entry_at(table, a), row) for a in anchors]
            high, low, us, ws = energy_pair(owns, fars)
            push = pushes(high, low, owns, ws)
            react = reactions(high, low, fars, us)
            for k in range(2):
                force[targets[k]] += push[k][0:3]
                force[anchors[k]] += react[k][0:3]


def brick_kernel(border_pick, index, table, message, back, react_out):
    row = rows8()
    count = message.shape[0]

    @pl.loop(0, count // 4)
    def group(step):
        for half in range(2):
            first = step * 4 + half * 2
            owns, fars = [], []
            for k in range(2):
                got = index[first + k]
                anchor = border_pick[0, jnp.maximum(got, 0)]
                x = jnp.concatenate([message[first + k], jnp.zeros((4, 128), F32)], axis=0)
                square = jnp.where(row < 3, x * x, 0.0)
                level = -0.5 * jnp.sum(square, axis=0, keepdims=True) + jnp.where(got >= 0, 0.0, OFF)
                owns.append(jnp.where(row < 3, x, jnp.where(row == 3, level, jnp.where(row == 7, 1.0, 0.0))))
                fars.append(far_block(entry_at(table, anchor), row))
            high, low, us, ws = energy_pair(owns, fars)
            push = pushes(high, low, owns, ws)
            react = reactions(high, low, fars, us)
            for k in range(2):
                back[first + k] = push[k][0:3]
                react_out[first + k] = react[k][0:3]


def face_kernel(flags, sent_lo, got_lo, sent_hi, got_hi, push_out, react_out):
    row = rows8()
    facing = sent_lo.shape[0]
    for side, (sent, got) in enumerate(((sent_lo, got_lo), (sent_hi, got_hi))):

        @pl.when(flags[side] > 0)
        def work():
            @pl.loop(0, facing // 2)
            def group(step):
                first = step * 2
                mine = [sent[first + k] for k in range(2)]
                theirs = [got[first + k] for k in range(2)]
                owns = [own_block(e, row) for e in mine]
                high, low, us, ws = energy_pair(owns, [far_block(e, row) for e in theirs])
                push = pushes(high, low, owns, ws)
                fars = [far_block(e, row) for e in mine]
                high, low, us, ws = energy_pair([own_block(e, row) for e in theirs], fars)
                react = reactions(high, low, fars, us)
                for k in range(2):
                    push_out[side, first + k] = push[k][0:3]
                    react_out[side, first + k] = react[k][0:3]


def final_kernel(
    flags, recv_pair, border_pick, index, face_pick, face_pair,
    force_in, brick_push, brick_react, face_push, face_react, force,
):
    force[...] = force_in[...]
    bricks, slots = recv_pair.shape[1], recv_pair.shape[2]

    @pl.loop(0, bricks)
    def brick(s):
        for k in range(slots):
            slot = s * slots + k
            target = recv_pair[0, s, k]

            @pl.when(target >= 0)
            def add():
                force[target] += brick_push[slot]

            got = index[slot]

            @pl.when(got >= 0)
            def add():
                force[border_pick[0, got]] += brick_react[slot]

    facing = face_pick.shape[2]
    for side in range(2):

        @pl.when(flags[side] > 0)
        def work():
            @pl.loop(0, facing, unroll=2)
            def face(k):
                force[jnp.maximum(face_pair[0, side, k], 0)] += face_push[side, k]
                force[face_pick[0, side, k]] += face_react[side, k]


SMEM = pl.BlockSpec(memory_space=pltpu.SMEM)
VMEM = pl.BlockSpec(memory_space=pltpu.VMEM)
HBM = pl.BlockSpec(memory_space=pl.ANY)


def call(kernel, out, in_specs, out_specs, scratch=(), aliases=None, cost=(0, 0, 0)):
    return pl.pallas_call(
        kernel,
        out_shape=out,
        in_specs=in_specs,
        out_specs=out_specs,
        scratch_shapes=list(scratch),
        input_output_aliases=aliases or {},
        compiler_params=pltpu.CompilerParams(vmem_limit_bytes=VMEM_LIMIT),
        cost_estimate=pl.CostEstimate(flops=cost[0], bytes_accessed=cost[1], transcendentals=cost[2]),
    )


def shape(*dims):
    return jax.ShapeDtypeStruct(dims, F32)


def body(verts, stiffness, local_pairs, border_pick, recv_src, recv_pair, face_pick, face_pair):
    patches = verts.shape[0]
    bricks, slots = recv_pair.shape[1], recv_pair.shape[2]
    facing = face_pick.shape[2]
    count = bricks * slots
    layer = lax.axis_index("slab")
    layers = lax.axis_size("slab")
    flags = jnp.stack([layer > 0, layer < layers - 1]).astype(jnp.int32)

    table, brick_msg, face_lo, face_hi = call(
        pack_kernel,
        (shape(patches * 8, 128), shape(count, 4, 128), shape(facing, 8, 128), shape(facing, 8, 128)),
        [SMEM] * 5 + [HBM, VMEM],
        (VMEM,) * 4,
        scratch=[pltpu.VMEM((3, patches, 128), F32), pltpu.SemaphoreType.DMA((3,))],
        cost=(patches * 128 * 60, patches * 128 * 48, 0),
    )(flags, recv_src, recv_pair, face_pick, face_pair, verts, stiffness)

    arrived = lax.all_to_all(brick_msg, "brick", 0, 0, tiled=True)
    got_hi = lax.ppermute(face_lo, "slab", [(i + 1, i) for i in range(layers - 1)])
    got_lo = lax.ppermute(face_hi, "slab", [(i, i + 1) for i in range(layers - 1)])

    pairs = local_pairs.shape[2]
    tile = 128 * 128
    force = call(
        local_kernel,
        shape(patches, 3, 128),
        [SMEM, VMEM],
        VMEM,
        cost=(pairs * tile * 400, patches * 128 * 44, pairs * tile),
    )(local_pairs, table)

    index = arrived[:, 3, 0].astype(jnp.int32)
    back, brick_react = call(
        brick_kernel,
        (shape(count, 3, 128), shape(count, 3, 128)),
        [SMEM, SMEM, VMEM, VMEM],
        (VMEM, VMEM),
        cost=(count * tile * 400, patches * 128 * 32, count * tile),
    )(border_pick, index, table, arrived)

    brick_push = lax.all_to_all(back, "brick", 0, 0, tiled=True)
    face_push, face_react = call(
        face_kernel,
        (shape(2, facing, 3, 128), shape(2, facing, 3, 128)),
        [SMEM, VMEM, VMEM, VMEM, VMEM],
        (VMEM, VMEM),
        cost=(4 * facing * tile * 400, facing * 128 * 4 * 44, 4 * facing * tile),
    )(flags, face_lo, got_lo, face_hi, got_hi)

    return call(
        final_kernel,
        shape(patches, 3, 128),
        [SMEM] * 6 + [VMEM] * 5,
        VMEM,
        cost=(facing * 128 * 24, patches * 128 * 24, 0),
    )(
        flags, recv_pair, border_pick, index, face_pick, face_pair,
        force, brick_push, brick_react, face_push, face_react,
    )


def solution(mesh):
    placed = (
        P(("slab", "brick"), None, None),
        P(("slab", "brick"), None),
        P(("slab", "brick"), None, None),
        P(("slab", "brick"), None),
        P(("slab", "brick"), None, None),
        P(("slab", "brick"), None, None),
        P(("slab", "brick"), None, None),
        P(("slab", "brick"), None, None),
    )
    return jax.shard_map(
        body,
        mesh=mesh,
        in_specs=placed,
        out_specs=P(("slab", "brick"), None, None),
        check_vma=False,
    )
```

time: 398 us -> 123 us (0.31); the launches traced: 392 us -> 121 us
  matrix products: 163 us -> 0 us
  local copies, waits for them, and re-layouts: 110 us -> 9.31 us
  Pallas kernels: 0 us -> 94 us
  other arithmetic: 91.2 us -> 1.31 us
  between operations: 14.3 us -> 0.13 us
  starting transfers between devices: 11.2 us -> 16.6 us
    dot_general x84 -> x0, matrix products: 163 us -> none  [the longest x28 67.2 us: tile_forces(): jnp.einsum('pci,pcj->pij', own_points, far_centres, precision=highest)]
    pallas_call x0 -> x5, Pallas kernels: none -> 94 us  [the longest x1 41.8 us: body(): call(local_kernel, shape(patches, 3, 128), [SMEM, VMEM], VMEM, cost=(pair...]
    gather x65 -> x0, local copies, waits for them, and re-layouts: 85.9 us -> none  [the longest x16 34.9 us: local_tiles(): centres[anchor_idx]]
    scatter-add x8 -> x0, other arithmetic: 74.3 us -> none  [the longest x1 25.1 us: body(): pushed = jnp.zeros_like(verts).at[target_loc].add(push_loc)]
    all_to_all x0 -> x2, starting transfers between devices: none -> 11.3 us  [the longest x1 5.66 us: body(): brick_push = lax.all_to_all(back, 'brick', 0, 0, tiled=True)]
    slice x30 -> x0, local copies, waits for them, and re-layouts: 9.92 us -> none  [the longest x13 3.46 us: centroids(): jnp.roll(points, -1, axis=-1)]
    div x2 -> x0, other arithmetic: 9.54 us -> none  [the longest x1 6.17 us: centroids(): (points + jnp.roll(points, -1, axis=-1) + jnp.roll(points, -2, axis=-1))...]
    unnamed x24 -> x25, local copies, waits for them, and re-layouts: 1.64 us -> 8.07 us
  transfers between devices with their start and end apart: 6 -> 4, of which waited for: 0 -> 0; matrix products, arithmetic and copies ran while one was open for 64% -> 1% of each run, Pallas kernels for 0% -> 68%
where the time goes in v1:
time: 123 us; the launch traced here: 121 us
  Pallas kernels  94 us (76%)
  starting transfers between devices  16.6 us (13%)
  local copies, waits for them, and re-layouts  9.31 us (8%)
  other arithmetic  1.31 us (1%)
    pallas_call x1, Pallas kernels, body(): call(local_kernel, shape(patches, 3, 128), [SMEM, VMEM], VMEM, cost=(pair...  41.8 us
    pallas_call x1, Pallas kernels, body(): call(face_kernel, (shape(2, facing, 3, 128), shape(2, facing, 3, 128)), [...  30 us
    pallas_call x1, Pallas kernels, body(): call(brick_kernel, (shape(count, 3, 128), shape(count, 3, 128)), [SMEM, S...  11.1 us
    unnamed x25, local copies, waits for them, and re-layouts  8.07 us
    pallas_call x1, Pallas kernels, body(): call(pack_kernel, (shape(patches * 8, 128), shape(count, 4, 128), shape(f...  7.88 us
    all_to_all x1, starting transfers between devices, body(): brick_push = lax.all_to_all(back, 'brick', 0, 0, tiled=True)  5.66 us
    all_to_all x1, starting transfers between devices, body(): arrived = lax.all_to_all(brick_msg, 'brick', 0, 0, tiled=True)  5.65 us
    pallas_call x1, Pallas kernels, body(): call(final_kernel, shape(patches, 3, 128), [SMEM] * 6 + [VMEM] * 5, VMEM,...  3.25 us
  transfers between devices with their start and end apart: 4, of which 0 were waited for; matrix products, arithmetic and copies ran while one was open for 1% of the time, Pallas kernels for 68%

profile of v1, /device:TPU:11, one launch (start us, length us, event | category | flops | bytes accessed | tf_op | source)
XLA Modules:
  0.0 121.4 jit_solution(17737778454735171272)
XLA Ops:
  0.0 0.0 copy-start.4
  0.0 0.0 copy-start.1
  0.0 2.5 %copy.11.verts = f32[1024,3,128]{2,1,0:T(4,128)S(1)} copy(f32[1024,3,128]{2,0,1:T(8,128)} %param.8) | data formatting | bytes 3145728 | tf_op args[0]
  2.6 0.0 copy-start.6
  2.6 0.1 add_convert_fusion.flags
  2.7 0.0 copy-done.5
  2.7 0.0 copy-done.2
  2.7 0.0 copy-done.3
  2.7 0.0 copy-done.4
  2.7 0.0 copy-done.1
  2.7 7.9 %shard_map.82 = (f32[8192,128]{1,0:T(8,128)}, f32[64,4,128]{2,1,0:T(4,128)}, f32[64,8,128]{2,1,0:T(8,128)S(1)}, f32[64,8,128]{2,1,0:T(8,128)S(1)}) custom-call(s32[2]{0:T(128)S(1)} %add_convert_fusion.flags, s32[1,8,8]{2,1,0:T(8,128)S(1)} %copy-done.5, s32[1,8,8]{2,1,0:T(8,128)S(1)} %copy-done.2, s32[1,2,64]{2,1,0:T(2,128)S(1)} %copy-done.3, ...), custom_call_target="tpu_custom_call" | custom-call | flops 7864320 | bytes 6291456 | tf_op jit(solution)/shard_map/pallas_call | solution.py:274
  10.6 5.6 %all-to-all-start = ((f32[64,4,128]{2,1,0:T(4,128)}), f32[64,4,128]{2,1,0:T(4,128)S(1)}, u32[]{:S(2)}, u32[]{:S(2)}) async-start(f32[64,4,128]{2,1,0:T(4,128)} %get-tuple-element.13), calls=%async_computation | async-start | bytes 262144 | tf_op jit(solution)/shard_map/all_to_all | solution.py:283
  16.2 3.1 %collective-permute-start = (f32[64,8,128]{2,1,0:T(8,128)S(1)}, f32[64,8,128]{2,1,0:T(8,128)S(1)}, u32[]{:S(2)}, u32[]{:S(2)}) collective-permute-start(f32[64,8,128]{2,1,0:T(8,128)S(1)} %get-tuple-element.18.sent_hi), channel_id=1, source_target_pairs={{0,8},{8,16},{16,24},{1,9},{9,17},{17,25},{2,10},{10,18},{18,26},{... | collective-permute-start | bytes 786440 | tf_op jit(solution)/shard_map/ppermute | solution.py:285
  19.4 2.2 %collective-permute-start.1 = (f32[64,8,128]{2,1,0:T(8,128)S(1)}, f32[64,8,128]{2,1,0:T(8,128)S(1)}, u32[]{:S(2)}, u32[]{:S(2)}) collective-permute-start(f32[64,8,128]{2,1,0:T(8,128)S(1)} %get-tuple-element.17.sent_lo), channel_id=1, source_target_pairs={{8,0},{16,8},{24,16},{9,1},{17,9},{25,17},{10,2},{18,10},{26,18},{... | collective-permute-start | bytes 786440 | tf_op jit(solution)/shard_map/ppermute | solution.py:284
  21.5 0.0 all-to-all-done.message
  21.6 1.2 %fusion.index = s32[64]{0:T(128)S(1)} fusion(f32[64,4,128]{2,1,0:T(4,128)S(1)} %all-to-all-done.message), kind=kLoop, calls=%fused_computation.1 | loop fusion | flops 64 | bytes 512 | tf_op jit(solution)/shard_map/convert_element_type | solution.py:297
  22.8 0.0 copy-done.6
  22.8 2.2 %copy-done = f32[8192,128]{1,0:T(8,128)S(1)} copy-done((f32[8192,128]{1,0:T(8,128)S(1)}, f32[8192,128]{1,0:T(8,128)}, u32[]{:S(2)}) %copy-start) | copy-done | bytes 4194328
  25.0 11.1 %shard_map.84 = (f32[64,3,128]{2,1,0:T(4,128)}, f32[64,3,128]{2,1,0:T(4,128)S(1)}) custom-call(s32[1,128]{1,0:T(1,128)S(1)} %copy-done.6, s32[64]{0:T(128)S(1)} %fusion.index, f32[8192,128]{1,0:T(8,128)S(1)} %copy-done, f32[64,4,128]{2,1,0:T(4,128)S(1)} %all-to-all-done.message), custom_call_target="tpu_custom_call" | custom-call | flops 419430400 | bytes 4194304 | tf_op jit(solution)/shard_map/pallas_call | solution.py:298
  36.1 5.7 %all-to-all-start.1 = ((f32[64,3,128]{2,1,0:T(4,128)}), f32[64,3,128]{2,1,0:T(4,128)S(1)}, u32[]{:S(2)}, u32[]{:S(2)}) async-start(f32[64,3,128]{2,1,0:T(4,128)} %get-tuple-element.15), calls=%async_computation.1 | async-start | bytes 262144 | tf_op jit(solution)/shard_map/all_to_all | solution.py:306
  41.8 41.8 %shard_map.83.force_in = f32[1024,3,128]{2,1,0:T(4,128)S(1)} custom-call(s32[1,2,256]{2,1,0:T(2,128)S(1)} %copy-done.11, f32[8192,128]{1,0:T(8,128)} %get-tuple-element.14.table), custom_call_target="tpu_custom_call" | custom-call | flops 1677721600 | bytes 5767168 | tf_op jit(solution)/shard_map/pallas_call | solution.py:289
  83.5 0.0 collective-permute-done.got_lo
  83.5 0.0 copy-start.7
  83.6 0.7 copy-done.7
  84.2 0.0 collective-permute-done.1.got_hi
  84.3 0.7 copy-done.9
  85.0 0.9 copy-done.8
  85.9 0.9 copy-done.10
  86.9 30.0 %shard_map.85 = (f32[2,64,3,128]{3,2,1,0:T(4,128)S(1)}, f32[2,64,3,128]{3,2,1,0:T(4,128)S(1)}) custom-call(s32[2]{0:T(128)S(1)} %add_convert_fusion.flags, f32[64,8,128]{2,1,0:T(8,128)S(1)} %get-tuple-element.17.sent_lo, f32[64,8,128]{2,1,0:T(8,128)S(1)} %copy-done.8, f32[64,8,128]{2,1,0:T(8,128)S(1)} %get-tuple-element.18.sent_hi, f32[64,8,128]{2,1,0:T(8,128)S(1)} %copy-done.10), custom_call_target="tpu_custom_call" | custom-call | flops 1677721600 | bytes 1441792 | tf_op jit(solution)/shard_map/pallas_call | solution.py:307
  116.9 0.0 all-to-all-done.1.brick_push
  116.9 3.2 %shard_map.86 = f32[1024,3,128]{2,1,0:T(4,128)S(1)} custom-call(s32[2]{0:T(128)S(1)} %add_convert_fusion.flags, s32[1,8,8]{2,1,0:T(8,128)S(1)} %copy-done.2, s32[1,128]{1,0:T(1,128)S(1)} %copy-done.6, s32[64]{0:T(128)S(1)} %fusion.index, s32[1,2,64]{2,1,0:T(2,128)S(1)} %copy-done.3, s32[1,2,64]{2,1,0:T(2,128)S(1)} %copy-done.4, ...), custom_call_target="tpu_custom_call" | custom-call | flops 196608 | bytes 3145728 | tf_op jit(solution)/shard_map/pallas_call | solution.py:315
  120.1 1.2 %copy.12 = f32[1024,3,128]{2,0,1:T(8,128)} copy(f32[1024,3,128]{2,1,0:T(4,128)S(1)} %shard_map.86) | data formatting | bytes 3145728 | tf_op jit(solution)/shard_map/pallas_call | solution.py:315
  (9 shorter events, 0.0 us)
Async XLA Ops:
  0.0 2.7 %copy-start.5 = (s32[1,8,8]{2,1,0:T(8,128)S(1)}, s32[1,8,8]{2,1,0:T(8,128)}, u32[]{:S(2)}) copy-start(s32[1,8,8]{2,1,0:T(8,128)} %recv_src.1) | copy-start | bytes 772
  0.0 2.7 %copy-start.2 = (s32[1,8,8]{2,1,0:T(8,128)S(1)}, s32[1,8,8]{2,1,0:T(8,128)}, u32[]{:S(2)}) copy-start(s32[1,8,8]{2,1,0:T(8,128)} %recv_pair.3) | copy-start | bytes 772
  0.0 2.7 %copy-start.3 = (s32[1,2,64]{2,1,0:T(2,128)S(1)}, s32[1,2,64]{2,1,0:T(2,128)}, u32[]{:S(2)}) copy-start(s32[1,2,64]{2,1,0:T(2,128)} %face_pick.3) | copy-start | bytes 1540
  0.0 2.7 %copy-start.4 = (s32[1,2,64]{2,1,0:T(2,128)S(1)}, s32[1,2,64]{2,1,0:T(2,128)}, u32[]{:S(2)}) copy-start(s32[1,2,64]{2,1,0:T(2,128)} %face_pair.3) | copy-start | bytes 1540
  0.0 2.7 %copy-start.1 = (f32[1024,128]{1,0:T(8,128)S(1)}, f32[1024,128]{1,0:T(8,128)}, u32[]{:S(2)}) copy-start(f32[1024,128]{1,0:T(8,128)} %stiffness.1) | copy-start | bytes 1572868
  2.6 20.2 %copy-start.6 = (s32[1,128]{1,0:T(1,128)S(1)}, s32[1,128]{1,0:T(1,128)}, u32[]{:S(2)}) copy-start(s32[1,128]{1,0:T(1,128)} %border_pick.3) | copy-start | bytes 1540
  10.6 11.0 %all-to-all-start = ((f32[64,4,128]{2,1,0:T(4,128)}), f32[64,4,128]{2,1,0:T(4,128)S(1)}, u32[]{:S(2)}, u32[]{:S(2)}) async-start(f32[64,4,128]{2,1,0:T(4,128)} %get-tuple-element.13), calls=%async_computation | async-start | bytes 262144 | tf_op jit(solution)/shard_map/all_to_all | solution.py:283
  16.2 67.3 %collective-permute-start = (f32[64,8,128]{2,1,0:T(8,128)S(1)}, f32[64,8,128]{2,1,0:T(8,128)S(1)}, u32[]{:S(2)}, u32[]{:S(2)}) collective-permute-start(f32[64,8,128]{2,1,0:T(8,128)S(1)} %get-tuple-element.18.sent_hi), channel_id=1, source_target_pairs={{0,8},{8,16},{16,24},{1,9},{9,17},{17,25},{2,10},{10,18},{18,26},{... | collective-permute-start | bytes 786440 | tf_op jit(solution)/shard_map/ppermute | solution.py:285
  19.4 64.9 %collective-permute-start.1 = (f32[64,8,128]{2,1,0:T(8,128)S(1)}, f32[64,8,128]{2,1,0:T(8,128)S(1)}, u32[]{:S(2)}, u32[]{:S(2)}) collective-permute-start(f32[64,8,128]{2,1,0:T(8,128)S(1)} %get-tuple-element.17.sent_lo), channel_id=1, source_target_pairs={{8,0},{16,8},{24,16},{9,1},{17,9},{25,17},{10,2},{18,10},{26,18},{... | collective-permute-start | bytes 786440 | tf_op jit(solution)/shard_map/ppermute | solution.py:284
  22.8 2.2 %copy-start = (f32[8192,128]{1,0:T(8,128)S(1)}, f32[8192,128]{1,0:T(8,128)}, u32[]{:S(2)}) copy-start(f32[8192,128]{1,0:T(8,128)} %get-tuple-element.14.table) | copy-start | bytes 12582916
  25.0 16.8 %copy-start.11 = (s32[1,2,256]{2,1,0:T(2,128)S(1)}, s32[1,2,256]{2,1,0:T(2,128)}, u32[]{:S(2)}) copy-start(s32[1,2,256]{2,1,0:T(2,128)} %local_pairs.1) | copy-start | bytes 6148
  36.1 80.8 %all-to-all-start.1 = ((f32[64,3,128]{2,1,0:T(4,128)}), f32[64,3,128]{2,1,0:T(4,128)S(1)}, u32[]{:S(2)}, u32[]{:S(2)}) async-start(f32[64,3,128]{2,1,0:T(4,128)} %get-tuple-element.15), calls=%async_computation.1 | async-start | bytes 262144 | tf_op jit(solution)/shard_map/all_to_all | solution.py:306
  83.5 0.7 copy-start.7
  84.3 0.7 copy-start.9
  85.0 0.9 copy-start.8
  85.9 0.9 copy-start.10

commit v2 on v0

v2 whole, which is shorter than its diff:
```python
import math

import jax
import jax.numpy as jnp
from jax import lax
from jax.experimental import pallas as pl
from jax.experimental.pallas import tpu as pltpu
from jax.sharding import PartitionSpec as P

F32 = jnp.float32
BF16 = jnp.bfloat16
ALPHA = math.sqrt(math.log2(math.e))
PUSH = 1.0 / ALPHA
REACT = 1.0 / (3.0 * ALPHA)
OFF = -1.0e5
VMEM_LIMIT = 64 * 1024 * 1024
WIDTH = 8
MATMUL = (((1,), (0,)), ((), ()))


def row_index():
    return lax.broadcasted_iota(jnp.int32, (8, 128), 0)


def split3(x):
    high = x.astype(BF16).astype(F32)
    rest = x - high
    mid = rest.astype(BF16).astype(F32)
    return high, mid, rest - mid


def own_block(entry, row):
    return jnp.where(row < 4, entry, jnp.where(row == 7, 1.0, pltpu.roll(entry, 4, 0)))


def far_block(entry, row):
    return jnp.where(row < 3, pltpu.roll(entry, 4, 0), jnp.where(row == 3, 1.0, entry))


def own_rows(parts, row):
    high, mid, low = parts
    one = jnp.where(row == 7, 1.0, 0.0)
    return [high, mid + one, jnp.where(row < 3, high, low) + one]


def far_rows(parts, row):
    high, mid, low = parts
    copy = (row >= 4) & (row < 7)
    return [
        jnp.where(copy, mid, high),
        jnp.where(row < 4, high, mid),
        jnp.where((row >= 3) & (row < 7), high, low),
    ]


def entry_at(ref, index):
    return ref[pl.ds(pl.multiple_of(index * 8, 8), 8), :]


def add_at(ref, index, value):
    ref[pl.ds(pl.multiple_of(index * 8, 8), 8), :] += value


def spread(react):
    return react + pltpu.roll(react, 1, 1) + pltpu.roll(react, 2, 1)


def tile_scratch(width):
    return [
        pltpu.VMEM((2 * width, 128, 48), BF16),
        pltpu.VMEM((2 * width, 48, 256), BF16),
        pltpu.VMEM((2 * width, 32, 128), BF16),
        pltpu.VMEM((2 * width, 128, 256), BF16),
        pltpu.VMEM((2 * width, 128, 256), BF16),
    ]


def run_tiles(start, stop, width, load, finish, scratch):
    lefts, rights, thins, highs, lows = scratch
    row = row_index()

    def prepare(n, slot):
        (far_down, own_down), (own_across, far_across) = load(n)
        left = far_rows(far_down, row) + own_rows(own_down, row)
        empty = [jnp.zeros((8, 128), F32)] * 3
        first = jnp.concatenate(own_rows(own_across, row) + empty, axis=0)
        second = jnp.concatenate(empty + far_rows(far_across, row), axis=0)
        lefts[slot] = jnp.concatenate(left, axis=0).astype(BF16).T
        rights[slot] = jnp.concatenate([first, second], axis=1).astype(BF16)
        thin = jnp.concatenate([far_down[0], far_down[1], own_down[0], own_down[1]], axis=0)
        thins[slot] = thin.astype(BF16)

    def energies(slot):
        energy = jnp.exp2(lax.dot_general(lefts[slot], rights[slot], MATMUL, preferred_element_type=F32))
        high = energy.astype(BF16)
        highs[slot] = high
        lows[slot] = (energy - high.astype(F32)).astype(BF16)

    def totals(slot):
        tall = jnp.concatenate([highs[slot], lows[slot]], axis=0)
        thin = jnp.concatenate([thins[slot], thins[slot]], axis=1)
        result = lax.dot_general(thin, tall, MATMUL, preferred_element_type=F32)
        push = result[0:8, 0:128] + result[8:16, 0:128]
        react = result[16:24, 128:256] + result[24:32, 128:256]
        return push, react

    last = stop - 1
    for q in range(2 * width):
        prepare(jnp.minimum(start + q, last), q)
    for q in range(width):
        energies(q)

    @pl.loop(0, (stop - start) // (2 * width))
    def step(m):
        base = start + m * (2 * width)
        for half in range(2):
            here, there = half * width, (1 - half) * width
            for q in range(width):
                finish(base + here + q, *totals(here + q))
                energies(there + q)
                prepare(jnp.minimum(base + 2 * width + here + q, last), here + q)


def push_of(own, total):
    return (own * total[3:4] - total) * PUSH


def react_of(far, total):
    return spread((far * total[7:8] - total) * REACT)


def width_for(couples):
    return math.gcd(couples, 2 * WIDTH) // 2


def build_table(verts, stiffness, table, first, last):
    @pl.loop(first // 8, last // 8, unroll=4)
    def build(step):
        base = pl.multiple_of(step * 8, 8)
        xs = [verts[c, pl.ds(base, 8), :] * ALPHA for c in range(3)]
        cs = [(x + pltpu.roll(x, 127, 1) + pltpu.roll(x, 126, 1)) * (1.0 / 3.0) for x in xs]
        strength = stiffness[pl.ds(base, 8), :]
        own = -0.5 * (xs[0] * xs[0] + xs[1] * xs[1] + xs[2] * xs[2])
        far = jnp.log2(strength) - 7.0 - 0.5 * (cs[0] * cs[0] + cs[1] * cs[1] + cs[2] * cs[2])
        for k, value in enumerate(xs + [own] + cs + [far]):
            table[pl.ds(step * 64 + k, 8, stride=8), :] = value


def clear_rows(ref):
    @pl.loop(0, ref.shape[0] // 64)
    def clear(n):
        ref[pl.ds(pl.multiple_of(n * 64, 64), 64), :] = jnp.zeros((64, 128), F32)


def message_index(message, index, sem):
    bricks = index.shape[0]
    slots = message.shape[0] // bricks
    return [
        pltpu.make_async_copy(message.at[s * slots, pl.ds(3, 1)], index.at[pl.ds(s, 1)], sem.at[s])
        for s in range(bricks)
    ]


def start_all(copies):
    for copy in copies:
        copy.start()
    return copies


def wait_all(copies):
    for copy in copies:
        copy.wait()


def copies_of(pairs, sem, first=0):
    return [pltpu.make_async_copy(source, target, sem.at[first + n]) for n, (source, target) in enumerate(pairs)]


def pack_kernel(
    border_any, src_any, pair_any, pick_any, facing_any, verts_any, stiffness_any,
    table_any, brick_any, lo_any, hi_any, border_out,
    border_pick, recv_src, recv_pair, face_pick, face_pair, verts, stiffness, table,
    brick_msg, face_lo, face_hi, border, small_sem, large_sem, out_sem, table_sem,
):
    patches = stiffness.shape[0]
    row = row_index()
    parts = table_sem.shape[0]
    rows = patches // parts
    large = []
    for part in range(parts):
        here = pl.ds(part * rows, rows)
        pieces = ((verts_any.at[:, here, :], verts.at[:, here, :]), (stiffness_any.at[here], stiffness.at[here]))
        large.append(start_all(copies_of(pieces, large_sem, 2 * part)))
    small = (
        (border_any, border_pick), (src_any, recv_src), (pair_any, recv_pair),
        (pick_any, face_pick), (facing_any, face_pair),
    )
    small = start_all(copies_of(small, small_sem))
    sends = []
    for part in range(parts):
        wait_all(large[part])
        build_table(verts, stiffness, table, part * rows, (part + 1) * rows)
        here = pl.ds(part * rows * 8, rows * 8)
        sends += start_all([pltpu.make_async_copy(table.at[here], table_any.at[here], table_sem.at[part])])
    wait_all(small)

    @pl.loop(0, border.shape[0] // 8, unroll=8)
    def borders(n):
        border[pl.ds(pl.multiple_of(n * 8, 8), 8), :] = entry_at(table, border_pick[0, n])

    sends += start_all(copies_of([(border, border_out)], out_sem, 3))
    @pl.loop(0, face_lo.shape[0], unroll=4)
    def face(k):
        for side, out in ((0, face_lo), (1, face_hi)):
            target = face_pair[0, side, k]
            level = jnp.where(target >= 0, 0.0, OFF)
            own = entry_at(table, jnp.maximum(target, 0)) + jnp.where(row == 3, level, 0.0)
            out[k] = jnp.where(row < 4, own, entry_at(table, face_pick[0, side, k]))

    sends += start_all(copies_of([(face_lo, lo_any), (face_hi, hi_any)], out_sem, 1))

    lane = lax.broadcasted_iota(jnp.int32, (8, 128), 1)
    bricks, slots = recv_pair.shape[1], recv_pair.shape[2]

    @pl.loop(0, bricks)
    def brick(s):
        index = jnp.full((8, 128), -1.0, F32)
        for k in range(slots):
            wanted = jnp.where(recv_pair[0, s, k] >= 0, recv_src[0, s, k], -1).astype(F32)
            index = jnp.where(lane == k, wanted, index)
        for k in range(slots):
            entry = entry_at(table, jnp.maximum(recv_pair[0, s, k], 0))
            brick_msg[s * slots + k] = jnp.where(row == 3, index, entry)[0:4]

    sends += start_all(copies_of([(brick_msg, brick_any)], out_sem))

    wait_all(sends)


def write_planes(force, planes, planes_out, sem, before=None):
    parts = sem.shape[0]
    rows = planes.shape[1] // parts
    sends = []
    for part in range(parts):

        @pl.loop(part * rows // 8, (part + 1) * rows // 8, unroll=8)
        def unpack(n):
            here = pl.ds(pl.multiple_of(n * 8, 8), 8)
            for c in range(3):
                value = force[pl.ds(n * 64 + c, 8, stride=8), :]
                planes[c, here, :] = value if before is None else planes[c, here, :] + value

        here = pl.ds(part * rows, rows)
        sends += start_all([pltpu.make_async_copy(planes.at[:, here, :], planes_out.at[:, here, :], sem.at[part])])
    wait_all(sends)


def local_kernel(local_any, table_any, planes_out, local_pairs, table, force, planes, sem, plane_sem, *scratch):
    row = row_index()
    copies = start_all(copies_of([(local_any, local_pairs), (table_any, table)], sem))
    clear_rows(force)
    wait_all(copies)

    def load(n):
        own = split3(own_block(entry_at(table, local_pairs[0, 0, n]), row))
        far = split3(far_block(entry_at(table, local_pairs[0, 1, n]), row))
        return (far, own), (own, far)

    def finish(n, push, react):
        target, anchor = local_pairs[0, 0, n], local_pairs[0, 1, n]
        add_at(force, target, push_of(entry_at(table, target), push))
        add_at(force, anchor, react_of(pltpu.roll(entry_at(table, anchor), 4, 0), react))

    pairs = local_pairs.shape[2]
    run_tiles(0, pairs, width_for(pairs), load, finish, scratch)
    write_planes(force, planes, planes_out, plane_sem)


def brick_kernel(border_any, message_any, after_any, back_any, react_any, border, message, back, react_out, index, sem, *scratch):
    row = row_index()
    bricks = index.shape[0]
    count = message.shape[0]
    slots = count // bricks
    copies = message_index(message_any, index, sem)
    copies.append(pltpu.make_async_copy(border_any, border, sem.at[bricks]))
    copies.append(pltpu.make_async_copy(message_any, message, sem.at[bricks + 1]))
    for copy in copies:
        copy.start()
    for copy in copies:
        copy.wait()

    def blocks(n):
        wanted = index[n // slots, n % slots].astype(jnp.int32)
        x = jnp.concatenate([message[n], message[n]], axis=0)
        square = jnp.where(row < 3, x * x, 0.0)
        level = -0.5 * jnp.sum(square, axis=0, keepdims=True) + jnp.where(wanted >= 0, 0.0, OFF)
        own = jnp.where(row == 3, level, jnp.where(row == 7, 1.0, x))
        return own, far_block(entry_at(border, jnp.maximum(wanted, 0)), row)

    def load(n):
        own, far = (split3(block) for block in blocks(n))
        return (far, own), (own, far)

    def finish(n, push, react):
        own, far = blocks(n)
        back[n] = push_of(own, push)[0:4]
        react_out[pl.ds(pl.multiple_of(n * 8, 8), 8), :] = react_of(far, react)

    run_tiles(0, count, width_for(count), load, finish, scratch)
    copies = [
        pltpu.make_async_copy(back, back_any, sem.at[bricks]),
        pltpu.make_async_copy(react_out, react_any, sem.at[bricks + 1]),
    ]
    for copy in copies:
        copy.start()
    for copy in copies:
        copy.wait()


def face_kernel(
    border_any, pick_any, pair_any, message, react_any, planes_in, sent_lo, sent_hi, got_lo, got_hi,
    planes_out, border_pick, face_pick, face_pair, brick_react, planes, force, sent, got, index, sem, index_sem, plane_sem,
    *scratch,
):
    row = row_index()
    facing = face_pick.shape[2]
    bricks = index.shape[0]
    slots = message.shape[0] // bricks
    copies = message_index(message, index, index_sem)
    for side, (mine, theirs) in enumerate(((sent_lo, got_lo), (sent_hi, got_hi))):
        copies.append(pltpu.make_async_copy(mine, sent.at[side], sem.at[side]))
        copies.append(pltpu.make_async_copy(theirs, got.at[side], sem.at[side + 2]))
    for n, (source, target) in enumerate(
        ((border_any, border_pick), (pick_any, face_pick), (pair_any, face_pair), (react_any, brick_react))
    ):
        copies.append(pltpu.make_async_copy(source, target, sem.at[n + 4]))
    before = pltpu.make_async_copy(planes_in, planes, sem.at[8])
    for copy in copies + [before]:
        copy.start()
    clear_rows(force)
    for copy in copies:
        copy.wait()

    @pl.loop(0, bricks)
    def add_bricks(s):
        for k in range(slots):
            anchor = border_pick[0, jnp.maximum(index[s, k].astype(jnp.int32), 0)]
            add_at(force, anchor, entry_at(brick_react, s * slots + k))

    layer = lax.axis_index("slab")
    has_low, has_high = layer > 0, layer < lax.axis_size("slab") - 1

    def load(n):
        side, k = n // facing, n % facing
        mine, theirs = sent[side, k], got[side, k]
        down = split3(far_block(theirs, row)), split3(own_block(theirs, row))
        return down, (split3(own_block(mine, row)), split3(far_block(mine, row)))

    def finish(n, push, react):
        side, k = n // facing, n % facing
        mine = sent[side, k]
        add_at(force, jnp.maximum(face_pair[0, side, k], 0), push_of(mine, push))
        add_at(force, face_pick[0, side, k], react_of(pltpu.roll(mine, 4, 0), react))

    start = jnp.where(has_low, 0, facing)
    stop = jnp.where(has_high, 2 * facing, facing)
    run_tiles(start, stop, width_for(facing), load, finish, scratch)

    before.wait()
    write_planes(force, planes, planes_out, plane_sem, before)


def final_kernel(pair_any, planes_any, push_any, out_any, recv_pair, low, mid, high, brick_push, in_sem, out_sem):
    planes = (low, mid, high)
    small = start_all(copies_of(((push_any, brick_push), (pair_any, recv_pair)), in_sem, 3))
    large = start_all(copies_of([(planes_any.at[c], plane) for c, plane in enumerate(planes)], in_sem))
    bricks, slots = recv_pair.shape[1], recv_pair.shape[2]
    wait_all(small)
    sends = []
    for c, plane in enumerate(planes):
        large[c].wait()

        @pl.loop(0, bricks)
        def brick(s):
            for k in range(slots):
                target = recv_pair[0, s, k]
                push = jnp.where(target >= 0, brick_push[s * slots + k, c:c + 1], 0.0)
                plane[pl.ds(jnp.maximum(target, 0), 1), :] += push

        sends += start_all(copies_of([(plane, out_any.at[c])], out_sem, c))
    wait_all(sends)


HBM = pl.BlockSpec(memory_space=pltpu.HBM)


def call(kernel, out, in_specs, out_specs, scratch, cost):
    return pl.pallas_call(
        kernel,
        out_shape=out,
        in_specs=in_specs,
        out_specs=out_specs,
        scratch_shapes=scratch,
        compiler_params=pltpu.CompilerParams(vmem_limit_bytes=VMEM_LIMIT),
        cost_estimate=pl.CostEstimate(flops=cost[0], bytes_accessed=cost[1], transcendentals=cost[2]),
    )


def shape(*dims):
    return jax.ShapeDtypeStruct(dims, F32)


def body(verts, stiffness, local_pairs, border_pick, recv_src, recv_pair, face_pick, face_pair):
    patches = verts.shape[0]
    bricks, slots = recv_pair.shape[1], recv_pair.shape[2]
    facing = face_pick.shape[2]
    count = bricks * slots
    pairs = local_pairs.shape[2]
    layers = lax.axis_size("slab")
    tile = 128 * 128

    table, brick_msg, face_lo, face_hi, border = call(
        pack_kernel,
        (
            shape(patches * 8, 128), shape(count, 4, 128), shape(facing, 8, 128), shape(facing, 8, 128),
            shape(border_pick.shape[1] * 8, 128),
        ),
        [HBM] * 7,
        (HBM,) * 5,
        scratch=[pltpu.SMEM(array.shape, jnp.int32) for array in (border_pick, recv_src, recv_pair, face_pick, face_pair)]
        + [
            pltpu.VMEM((3, patches, 128), F32),
            pltpu.VMEM((patches, 128), F32),
            pltpu.VMEM((patches * 8, 128), F32),
            pltpu.VMEM((count, 4, 128), F32),
            pltpu.VMEM((facing, 8, 128), F32),
            pltpu.VMEM((facing, 8, 128), F32),
            pltpu.VMEM((border_pick.shape[1] * 8, 128), F32),
        ]
        + [pltpu.SemaphoreType.DMA((n,)) for n in (5, 8, 4, 4)],
        cost=(patches * 128 * 60, patches * 128 * 48, 0),
    )(
        border_pick, recv_src, recv_pair, face_pick, face_pair,
        jnp.transpose(verts, (1, 0, 2)), stiffness,
    )

    arrived = lax.all_to_all(brick_msg, "brick", 0, 0, tiled=True)
    got_hi = lax.ppermute(face_lo, "slab", [((i + 1) % layers, i) for i in range(layers)])
    got_lo = lax.ppermute(face_hi, "slab", [(i, (i + 1) % layers) for i in range(layers)])

    planes = call(
        local_kernel,
        shape(3, patches, 128),
        [HBM] * 2,
        HBM,
        scratch=[
            pltpu.SMEM(local_pairs.shape, jnp.int32),
            pltpu.VMEM((patches * 8, 128), F32),
            pltpu.VMEM((patches * 8, 128), F32),
            pltpu.VMEM((3, patches, 128), F32),
            pltpu.SemaphoreType.DMA((2,)),
            pltpu.SemaphoreType.DMA((4,)),
        ]
        + tile_scratch(WIDTH),
        cost=(pairs * tile * 400, patches * 128 * 48, pairs * tile),
    )(local_pairs, table)

    back, brick_react = call(
        brick_kernel,
        (shape(count, 4, 128), shape(count * 8, 128)),
        [HBM, HBM, HBM],
        (HBM, HBM),
        scratch=[
            pltpu.VMEM(border.shape, F32),
            pltpu.VMEM(arrived.shape, F32),
            pltpu.VMEM((count, 4, 128), F32),
            pltpu.VMEM((count * 8, 128), F32),
            pltpu.SMEM((bricks, 128), F32),
            pltpu.SemaphoreType.DMA((bricks + 2,)),
        ]
        + tile_scratch(WIDTH),
        cost=(count * tile * 400, patches * 128 * 32, count * tile),
    )(border, arrived, planes)

    brick_push = lax.all_to_all(back, "brick", 0, 0, tiled=True)
    planes = call(
        face_kernel,
        shape(3, patches, 128),
        [HBM] * 10,
        HBM,
        scratch=[
            pltpu.SMEM(border_pick.shape, jnp.int32),
            pltpu.SMEM(face_pick.shape, jnp.int32),
            pltpu.SMEM(face_pair.shape, jnp.int32),
            pltpu.VMEM((count * 8, 128), F32),
            pltpu.VMEM((3, patches, 128), F32),
            pltpu.VMEM((patches * 8, 128), F32),
            pltpu.VMEM((2, facing, 8, 128), F32),
            pltpu.VMEM((2, facing, 8, 128), F32),
            pltpu.SMEM((bricks, 128), F32),
            pltpu.SemaphoreType.DMA((9,)),
            pltpu.SemaphoreType.DMA((bricks,)),
            pltpu.SemaphoreType.DMA((4,)),
        ]
        + tile_scratch(WIDTH),
        cost=(4 * facing * tile * 400, patches * 128 * 64, 4 * facing * tile),
    )(border_pick, face_pick, face_pair, arrived, brick_react, planes, face_lo, face_hi, got_lo, got_hi)

    out = call(
        final_kernel,
        shape(3, patches, 128),
        [HBM, HBM, HBM],
        HBM,
        scratch=[pltpu.SMEM(recv_pair.shape, jnp.int32)]
        + [pltpu.VMEM((patches, 128), F32)] * 3
        + [pltpu.VMEM((count, 4, 128), F32), pltpu.SemaphoreType.DMA((5,)), pltpu.SemaphoreType.DMA((3,))],
        cost=(count * 128 * 24, patches * 128 * 24, 0),
    )(recv_pair, planes, brick_push)
    return jnp.transpose(out, (1, 0, 2))


def solution(mesh):
    placed = (
        P(("slab", "brick"), None, None),
        P(("slab", "brick"), None),
        P(("slab", "brick"), None, None),
        P(("slab", "brick"), None),
        P(("slab", "brick"), None, None),
        P(("slab", "brick"), None, None),
        P(("slab", "brick"), None, None),
        P(("slab", "brick"), None, None),
    )
    return jax.shard_map(
        body,
        mesh=mesh,
        in_specs=placed,
        out_specs=P(("slab", "brick"), None, None),
        check_vma=False,
    )
```

time: 398 us -> 51.7 us (0.13)
  the two profiles are of different devices: /device:TPU:11 before, /device:TPU:13 now
where the time goes in v2:
time: 51.7 us; the launch traced here: 51.2 us
  Pallas kernels  37.5 us (73%)
  starting transfers between devices  13.7 us (26%)
    pallas_call x1, Pallas kernels, body(): call(local_kernel, shape(3, patches, 128), [HBM] * 2, HBM, scratch=[pltpu...  14.1 us
    pallas_call x1, Pallas kernels, body(): call(face_kernel, shape(3, patches, 128), [HBM] * 10, HBM, scratch=[pltpu...  8.77 us
    pallas_call x1, Pallas kernels, body(): call(pack_kernel, (shape(patches * 8, 128), shape(count, 4, 128), shape(f...  6.18 us
    all_to_all x1, starting transfers between devices, body(): brick_push = lax.all_to_all(back, 'brick', 0, 0, tiled=True)  5.68 us
    all_to_all x1, starting transfers between devices, body(): arrived = lax.all_to_all(brick_msg, 'brick', 0, 0, tiled=True)  5.65 us
    pallas_call x1, Pallas kernels, body(): call(brick_kernel, (shape(count, 4, 128), shape(count * 8, 128)), [HBM, H...  5.31 us
    pallas_call x1, Pallas kernels, body(): call(final_kernel, shape(3, patches, 128), [HBM, HBM, HBM], HBM, scratch=...  3.08 us
    ppermute x1, starting transfers between devices, body(): lax.ppermute(face_hi, 'slab', [(i, (i + 1) % layers) for i in range(layer...  1.21 us
  transfers between devices with their start and end apart: 4, of which 0 were waited for; matrix products, arithmetic and copies ran while one was open for 0% of the time, Pallas kernels for 55%

profile of v2, /device:TPU:13, one launch (start us, length us, event | category | flops | bytes accessed | tf_op | source)
XLA Modules:
  0.0 51.2 jit_solution(1036159708689157949)
XLA Ops:
  0.0 6.2 %shard_map.82 = (f32[8192,128]{1,0:T(8,128)}, f32[64,4,128]{2,1,0:T(4,128)}, f32[64,8,128]{2,1,0:T(8,128)}, f32[64,8,128]{2,1,0:T(8,128)}, f32[1024,128]{1,0:T(8,128)}) custom-call(s32[1,128]{1,0:T(1,128)} %border_any.3, s32[1,8,8]{2,1,0:T(8,128)} %src_any.1, s32[1,8,8]{2,1,0:T(8,128)} %pair_any.5, s32[1,2,64]{2,1,0:T(2,128)} %pick_any.3, ...), custom_call_target="tpu_custom_call" | custom-call | flops 7864320 | bytes 6291456 | tf_op jit(solution)/shard_map/pallas_call | solution.py:422
  6.2 5.6 %all-to-all-start = ((f32[64,4,128]{2,1,0:T(4,128)}), f32[64,4,128]{2,1,0:T(4,128)}, u32[]{:S(2)}, u32[]{:S(2)}) async-start(f32[64,4,128]{2,1,0:T(4,128)} %get-tuple-element.12), calls=%async_computation | async-start | bytes 262144 | tf_op jit(solution)/shard_map/all_to_all | solution.py:447
  11.8 1.2 %collective-permute-start = (f32[64,8,128]{2,1,0:T(8,128)}, f32[64,8,128]{2,1,0:T(8,128)}, u32[]{:S(2)}, u32[]{:S(2)}) collective-permute-start(f32[64,8,128]{2,1,0:T(8,128)} %get-tuple-element.17.sent_hi), channel_id=1, source_target_pairs={{0,8},{8,16},{16,24},{24,0},{1,9},{9,17},{17,25},{25,1},{2,10},{10... | collective-permute-start | bytes 786440 | tf_op jit(solution)/shard_map/ppermute | solution.py:449
  13.0 1.2 %collective-permute-start.1 = (f32[64,8,128]{2,1,0:T(8,128)}, f32[64,8,128]{2,1,0:T(8,128)}, u32[]{:S(2)}, u32[]{:S(2)}) collective-permute-start(f32[64,8,128]{2,1,0:T(8,128)} %get-tuple-element.16.sent_lo), channel_id=1, source_target_pairs={{8,0},{16,8},{24,16},{0,24},{9,1},{17,9},{25,17},{1,25},{10,2},{18... | collective-permute-start | bytes 786440 | tf_op jit(solution)/shard_map/ppermute | solution.py:448
  14.2 14.1 %shard_map.83.after_any.planes_in = f32[3,1024,128]{2,1,0:T(8,128)} custom-call(s32[1,2,256]{2,1,0:T(2,128)} %local_any.1, f32[8192,128]{1,0:T(8,128)} %get-tuple-element.14.table_any), custom_call_target="tpu_custom_call" | custom-call | flops 1677721600 | bytes 6291456 | tf_op jit(solution)/shard_map/pallas_call | solution.py:451
  28.3 0.0 all-to-all-done.message_any.message
  28.3 5.3 %shard_map.84 = (f32[64,4,128]{2,1,0:T(4,128)}, f32[512,128]{1,0:T(8,128)}) custom-call(f32[1024,128]{1,0:T(8,128)} %get-tuple-element.13.border_any, f32[64,4,128]{2,1,0:T(4,128)} %all-to-all-done.message_any.message, f32[3,1024,128]{2,1,0:T(8,128)} %shard_map.83.after_any.planes_in), custom_call_target="tpu_custom_call" | custom-call | flops 419430400 | bytes 4194304 | tf_op jit(solution)/shard_map/pallas_call | solution.py:468
  33.7 5.7 %all-to-all-start.1 = ((f32[64,4,128]{2,1,0:T(4,128)}), f32[64,4,128]{2,1,0:T(4,128)}, u32[]{:S(2)}, u32[]{:S(2)}) async-start(f32[64,4,128]{2,1,0:T(4,128)} %get-tuple-element.18), calls=%async_computation.1 | async-start | bytes 262144 | tf_op jit(solution)/shard_map/all_to_all | solution.py:485
  39.3 0.0 collective-permute-done.got_lo
  39.3 0.0 collective-permute-done.1.got_hi
  39.4 8.8 %shard_map.85.planes_any = f32[3,1024,128]{2,1,0:T(8,128)} custom-call(s32[1,128]{1,0:T(1,128)} %border_any.3, s32[1,2,64]{2,1,0:T(2,128)} %pick_any.3, s32[1,2,64]{2,1,0:T(2,128)} %pair_any.4, f32[64,4,128]{2,1,0:T(4,128)} %all-to-all-done.message_any.message, f32[512,128]{1,0:T(8,128)} %get-tuple-element.15.react_any, ...), custom_call_target="tpu_custom_call" | custom-call | flops 1677721600 | bytes 8388608 | tf_op jit(solution)/shard_map/pallas_call | solution.py:486
  48.1 0.0 all-to-all-done.1.push_any
  48.1 3.1 %shard_map.86 = f32[3,1024,128]{2,1,0:T(8,128)} custom-call(s32[1,8,8]{2,1,0:T(8,128)} %pair_any.5, f32[3,1024,128]{2,1,0:T(8,128)} %shard_map.85.planes_any, f32[64,4,128]{2,1,0:T(4,128)} %all-to-all-done.1.push_any), custom_call_target="tpu_custom_call" | custom-call | flops 196608 | bytes 3145728 | tf_op jit(solution)/shard_map/pallas_call | solution.py:509
Async XLA Ops:
  6.2 22.1 %all-to-all-start = ((f32[64,4,128]{2,1,0:T(4,128)}), f32[64,4,128]{2,1,0:T(4,128)}, u32[]{:S(2)}, u32[]{:S(2)}) async-start(f32[64,4,128]{2,1,0:T(4,128)} %get-tuple-element.12), calls=%async_computation | async-start | bytes 262144 | tf_op jit(solution)/shard_map/all_to_all | solution.py:447
  11.8 27.5 %collective-permute-start = (f32[64,8,128]{2,1,0:T(8,128)}, f32[64,8,128]{2,1,0:T(8,128)}, u32[]{:S(2)}, u32[]{:S(2)}) collective-permute-start(f32[64,8,128]{2,1,0:T(8,128)} %get-tuple-element.17.sent_hi), channel_id=1, source_target_pairs={{0,8},{8,16},{16,24},{24,0},{1,9},{9,17},{17,25},{25,1},{2,10},{10... | collective-permute-start | bytes 786440 | tf_op jit(solution)/shard_map/ppermute | solution.py:449
  13.0 26.3 %collective-permute-start.1 = (f32[64,8,128]{2,1,0:T(8,128)}, f32[64,8,128]{2,1,0:T(8,128)}, u32[]{:S(2)}, u32[]{:S(2)}) collective-permute-start(f32[64,8,128]{2,1,0:T(8,128)} %get-tuple-element.16.sent_lo), channel_id=1, source_target_pairs={{8,0},{16,8},{24,16},{0,24},{9,1},{17,9},{25,17},{1,25},{10,2},{18... | collective-permute-start | bytes 786440 | tf_op jit(solution)/shard_map/ppermute | solution.py:448
  33.7 14.5 %all-to-all-start.1 = ((f32[64,4,128]{2,1,0:T(4,128)}), f32[64,4,128]{2,1,0:T(4,128)}, u32[]{:S(2)}, u32[]{:S(2)}) async-start(f32[64,4,128]{2,1,0:T(4,128)} %get-tuple-element.18), calls=%async_computation.1 | async-start | bytes 262144 | tf_op jit(solution)/shard_map/all_to_all | solution.py:485

commit v3 on v2

--- a/solution.py
+++ b/solution.py
@@ -72,11 +72,12 @@
         pltpu.VMEM((2 * width, 32, 128), BF16),
         pltpu.VMEM((2 * width, 128, 256), BF16),
         pltpu.VMEM((2 * width, 128, 256), BF16),
+        pltpu.VMEM((2 * width, 2, 8, 128), F32),
     ]
 
 
 def run_tiles(start, stop, width, load, finish, scratch):
-    lefts, rights, thins, highs, lows = scratch
+    lefts, rights, thins, highs, lows, sums = scratch
     row = row_index()
 
     def prepare(n, slot):
@@ -110,16 +111,22 @@
     for q in range(width):
         energies(q)
 
+    sums[width:] = jnp.zeros((width, 2, 8, 128), F32)
+
     @pl.loop(0, (stop - start) // (2 * width))
     def step(m):
         base = start + m * (2 * width)
         for half in range(2):
             here, there = half * width, (1 - half) * width
             for q in range(width):
-                finish(base + here + q, *totals(here + q))
+                finish(jnp.maximum(base + here + q - width, start), sums[there + q, 0], sums[there + q, 1])
+                sums[here + q, 0], sums[here + q, 1] = totals(here + q)
                 energies(there + q)
                 prepare(jnp.minimum(base + 2 * width + here + q, last), here + q)
 
+    for q in range(width):
+        finish(stop - width + q, sums[width + q, 0], sums[width + q, 1])
+
 
 def push_of(own, total):
     return (own * total[3:4] - total) * PUSH
@@ -134,7 +141,7 @@
 
 
 def build_table(verts, stiffness, table, first, last):
-    @pl.loop(first // 8, last // 8, unroll=4)
+    @pl.loop(first // 8, last // 8, unroll=32)
     def build(step):
         base = pl.multiple_of(step * 8, 8)
         xs = [verts[c, pl.ds(base, 8), :] * ALPHA for c in range(3)]
@@ -147,18 +154,13 @@
 
 
 def clear_rows(ref):
-    @pl.loop(0, ref.shape[0] // 64)
+    @pl.loop(0, ref.shape[0] // 64, unroll=8)
     def clear(n):
         ref[pl.ds(pl.multiple_of(n * 64, 64), 64), :] = jnp.zeros((64, 128), F32)
 
 
 def message_index(message, index, sem):
-    bricks = index.shape[0]
-    slots = message.shape[0] // bricks
-    return [
-        pltpu.make_async_copy(message.at[s * slots, pl.ds(3, 1)], index.at[pl.ds(s, 1)], sem.at[s])
-        for s in range(bricks)
-    ]
+    return pltpu.make_async_copy(message.at[:, 3, :], index, sem)
 
 
 def start_all(copies):
@@ -177,14 +179,14 @@
 
 
 def pack_kernel(
-    border_any, src_any, pair_any, pick_any, facing_any, verts_any, stiffness_any,
-    table_any, brick_any, lo_any, hi_any, border_out,
-    border_pick, recv_src, recv_pair, face_pick, face_pair, verts, stiffness, table,
-    brick_msg, face_lo, face_hi, border, small_sem, large_sem, out_sem, table_sem,
+    local_any, border_any, src_any, pair_any, pick_any, facing_any, verts_any, stiffness_any,
+    near_any, brick_any, lo_any, hi_any, border_out,
+    local_pairs, border_pick, recv_src, recv_pair, face_pick, face_pair, verts, stiffness, table, near,
+    brick_msg, face_lo, face_hi, border, small_sem, large_sem, out_sem,
 ):
     patches = stiffness.shape[0]
     row = row_index()
-    parts = table_sem.shape[0]
+    parts = large_sem.shape[0] // 2
     rows = patches // parts
     large = []
     for part in range(parts):
@@ -192,7 +194,7 @@
         pieces = ((verts_any.at[:, here, :], verts.at[:, here, :]), (stiffness_any.at[here], stiffness.at[here]))
         large.append(start_all(copies_of(pieces, large_sem, 2 * part)))
     small = (
-        (border_any, border_pick), (src_any, recv_src), (pair_any, recv_pair),
+        (local_any, local_pairs), (border_any, border_pick), (src_any, recv_src), (pair_any, recv_pair),
         (pick_any, face_pick), (facing_any, face_pair),
     )
     small = start_all(copies_of(small, small_sem))
@@ -200,37 +202,39 @@
     for part in range(parts):
         wait_all(large[part])
         build_table(verts, stiffness, table, part * rows, (part + 1) * rows)
-        here = pl.ds(part * rows * 8, rows * 8)
-        sends += start_all([pltpu.make_async_copy(table.at[here], table_any.at[here], table_sem.at[part])])
     wait_all(small)
 
-    @pl.loop(0, border.shape[0] // 8, unroll=8)
+    @pl.loop(0, near.shape[0] // 8, unroll=16)
+    def pairs(n):
+        own, far = entry_at(table, local_pairs[0, 0, n]), entry_at(table, local_pairs[0, 1, n])
+        near[pl.ds(pl.multiple_of(n * 8, 8), 8), :] = jnp.where(row < 4, own, far)
+
+    sends += start_all(copies_of([(near, near_any)], out_sem, 4))
+
+    @pl.loop(0, border.shape[0] // 8, unroll=16)
     def borders(n):
         border[pl.ds(pl.multiple_of(n * 8, 8), 8), :] = entry_at(table, border_pick[0, n])
 
     sends += start_all(copies_of([(border, border_out)], out_sem, 3))
-    @pl.loop(0, face_lo.shape[0], unroll=4)
+    @pl.loop(0, face_lo.shape[0] // 8, unroll=8)
     def face(k):
         for side, out in ((0, face_lo), (1, face_hi)):
             target = face_pair[0, side, k]
             level = jnp.where(target >= 0, 0.0, OFF)
             own = entry_at(table, jnp.maximum(target, 0)) + jnp.where(row == 3, level, 0.0)
-            out[k] = jnp.where(row < 4, own, entry_at(table, face_pick[0, side, k]))
+            out[pl.ds(pl.multiple_of(k * 8, 8), 8), :] = jnp.where(row < 4, own, entry_at(table, face_pick[0, side, k]))
 
     sends += start_all(copies_of([(face_lo, lo_any), (face_hi, hi_any)], out_sem, 1))
 
-    lane = lax.broadcasted_iota(jnp.int32, (8, 128), 1)
     bricks, slots = recv_pair.shape[1], recv_pair.shape[2]
 
-    @pl.loop(0, bricks)
+    @pl.loop(0, bricks, unroll=2)
     def brick(s):
-        index = jnp.full((8, 128), -1.0, F32)
         for k in range(slots):
-            wanted = jnp.where(recv_pair[0, s, k] >= 0, recv_src[0, s, k], -1).astype(F32)
-            index = jnp.where(lane == k, wanted, index)
-        for k in range(slots):
-            entry = entry_at(table, jnp.maximum(recv_pair[0, s, k], 0))
-            brick_msg[s * slots + k] = jnp.where(row == 3, index, entry)[0:4]
+            target = recv_pair[0, s, k]
+            wanted = jnp.where(target >= 0, recv_src[0, s, k], -1).astype(F32)
+            entry = entry_at(table, jnp.maximum(target, 0))
+            brick_msg[s * slots + k] = jnp.where(row == 3, wanted, entry)[0:4]
 
     sends += start_all(copies_of([(brick_msg, brick_any)], out_sem))
 
@@ -243,7 +247,7 @@
     sends = []
     for part in range(parts):
 
-        @pl.loop(part * rows // 8, (part + 1) * rows // 8, unroll=8)
+        @pl.loop(part * rows // 8, (part + 1) * rows // 8, unroll=32)
         def unpack(n):
             here = pl.ds(pl.multiple_of(n * 8, 8), 8)
             for c in range(3):
@@ -255,21 +259,21 @@
     wait_all(sends)
 
 
-def local_kernel(local_any, table_any, planes_out, local_pairs, table, force, planes, sem, plane_sem, *scratch):
+def local_kernel(local_any, near_any, planes_out, local_pairs, near, force, planes, sem, plane_sem, *scratch):
     row = row_index()
-    copies = start_all(copies_of([(local_any, local_pairs), (table_any, table)], sem))
+    copies = start_all(copies_of([(local_any, local_pairs), (near_any, near)], sem))
     clear_rows(force)
     wait_all(copies)
 
     def load(n):
-        own = split3(own_block(entry_at(table, local_pairs[0, 0, n]), row))
-        far = split3(far_block(entry_at(table, local_pairs[0, 1, n]), row))
+        entry = entry_at(near, n)
+        own, far = split3(own_block(entry, row)), split3(far_block(entry, row))
         return (far, own), (own, far)
 
     def finish(n, push, react):
-        target, anchor = local_pairs[0, 0, n], local_pairs[0, 1, n]
-        add_at(force, target, push_of(entry_at(table, target), push))
-        add_at(force, anchor, react_of(pltpu.roll(entry_at(table, anchor), 4, 0), react))
+        entry = entry_at(near, n)
+        add_at(force, local_pairs[0, 0, n], push_of(entry, push))
+        add_at(force, local_pairs[0, 1, n], react_of(pltpu.roll(entry, 4, 0), react))
 
     pairs = local_pairs.shape[2]
     run_tiles(0, pairs, width_for(pairs), load, finish, scratch)
@@ -278,38 +282,31 @@
 
 def brick_kernel(border_any, message_any, after_any, back_any, react_any, border, message, back, react_out, index, sem, *scratch):
     row = row_index()
-    bricks = index.shape[0]
     count = message.shape[0]
-    slots = count // bricks
-    copies = message_index(message_any, index, sem)
-    copies.append(pltpu.make_async_copy(border_any, border, sem.at[bricks]))
-    copies.append(pltpu.make_async_copy(message_any, message, sem.at[bricks + 1]))
-    for copy in copies:
-        copy.start()
-    for copy in copies:
-        copy.wait()
-
-    def blocks(n):
-        wanted = index[n // slots, n % slots].astype(jnp.int32)
+    copies = [message_index(message_any, index, sem.at[2])]
+    copies += copies_of(((border_any, border), (message_any, message)), sem)
+    wait_all(start_all(copies))
+
+    def far_entry(n):
+        return entry_at(border, jnp.maximum(index[n, 0].astype(jnp.int32), 0))
+
+    def load(n):
         x = jnp.concatenate([message[n], message[n]], axis=0)
         square = jnp.where(row < 3, x * x, 0.0)
-        level = -0.5 * jnp.sum(square, axis=0, keepdims=True) + jnp.where(wanted >= 0, 0.0, OFF)
-        own = jnp.where(row == 3, level, jnp.where(row == 7, 1.0, x))
-        return own, far_block(entry_at(border, jnp.maximum(wanted, 0)), row)
-
-    def load(n):
-        own, far = (split3(block) for block in blocks(n))
+        level = -0.5 * jnp.sum(square, axis=0, keepdims=True) + jnp.where(index[n, 0] >= 0.0, 0.0, OFF)
+        own = split3(jnp.where(row == 3, level, jnp.where(row == 7, 1.0, x)))
+        far = split3(far_block(far_entry(n), row))
         return (far, own), (own, far)
 
     def finish(n, push, react):
-        own, far = blocks(n)
-        back[n] = push_of(own, push)[0:4]
+        back[n] = push_of(message[n], push[0:4])
+        far = pltpu.roll(far_entry(n), 4, 0)
         react_out[pl.ds(pl.multiple_of(n * 8, 8), 8), :] = react_of(far, react)
 
     run_tiles(0, count, width_for(count), load, finish, scratch)
     copies = [
-        pltpu.make_async_copy(back, back_any, sem.at[bricks]),
-        pltpu.make_async_copy(react_out, react_any, sem.at[bricks + 1]),
+        pltpu.make_async_copy(back, back_any, sem.at[0]),
+        pltpu.make_async_copy(react_out, react_any, sem.at[1]),
     ]
     for copy in copies:
         copy.start()
@@ -319,17 +316,16 @@
 
 def face_kernel(
     border_any, pick_any, pair_any, message, react_any, planes_in, sent_lo, sent_hi, got_lo, got_hi,
-    planes_out, border_pick, face_pick, face_pair, brick_react, planes, force, sent, got, index, sem, index_sem, plane_sem,
+    planes_out, border_pick, face_pick, face_pair, brick_react, planes, force, sent, got, index, sem, plane_sem,
     *scratch,
 ):
     row = row_index()
     facing = face_pick.shape[2]
-    bricks = index.shape[0]
-    slots = message.shape[0] // bricks
-    copies = message_index(message, index, index_sem)
+    copies = [message_index(message, index, sem.at[9])]
     for side, (mine, theirs) in enumerate(((sent_lo, got_lo), (sent_hi, got_hi))):
-        copies.append(pltpu.make_async_copy(mine, sent.at[side], sem.at[side]))
-        copies.append(pltpu.make_async_copy(theirs, got.at[side], sem.at[side + 2]))
+        here = pl.ds(side * facing * 8, facing * 8)
+        copies.append(pltpu.make_async_copy(mine, sent.at[here], sem.at[side]))
+        copies.append(pltpu.make_async_copy(theirs, got.at[here], sem.at[side + 2]))
     for n, (source, target) in enumerate(
         ((border_any, border_pick), (pick_any, face_pick), (pair_any, face_pair), (react_any, brick_react))
     ):
@@ -341,24 +337,23 @@
     for copy in copies:
         copy.wait()
 
-    @pl.loop(0, bricks)
-    def add_bricks(s):
-        for k in range(slots):
-            anchor = border_pick[0, jnp.maximum(index[s, k].astype(jnp.int32), 0)]
-            add_at(force, anchor, entry_at(brick_react, s * slots + k))
+    @pl.loop(0, index.shape[0], unroll=8)
+    def add_bricks(n):
+        anchor = border_pick[0, jnp.maximum(index[n, 0].astype(jnp.int32), 0)]
+        add_at(force, anchor, entry_at(brick_react, n))
 
     layer = lax.axis_index("slab")
     has_low, has_high = layer > 0, layer < lax.axis_size("slab") - 1
 
     def load(n):
-        side, k = n // facing, n % facing
-        mine, theirs = sent[side, k], got[side, k]
+        mine, theirs = entry_at(sent, n), entry_at(got, n)
         down = split3(far_block(theirs, row)), split3(own_block(theirs, row))
         return down, (split3(own_block(mine, row)), split3(far_block(mine, row)))
 
     def finish(n, push, react):
-        side, k = n // facing, n % facing
-        mine = sent[side, k]
+        side = (n >= facing).astype(jnp.int32)
+        k = n - side * facing
+        mine = entry_at(sent, n)
         add_at(force, jnp.maximum(face_pair[0, side, k], 0), push_of(mine, push))
         add_at(force, face_pick[0, side, k], react_of(pltpu.roll(mine, 4, 0), react))
 
@@ -419,28 +414,29 @@
     layers = lax.axis_size("slab")
     tile = 128 * 128
 
-    table, brick_msg, face_lo, face_hi, border = call(
+    near, brick_msg, face_lo, face_hi, border = call(
         pack_kernel,
         (
-            shape(patches * 8, 128), shape(count, 4, 128), shape(facing, 8, 128), shape(facing, 8, 128),
+            shape(pairs * 8, 128), shape(count, 4, 128), shape(facing * 8, 128), shape(facing * 8, 128),
             shape(border_pick.shape[1] * 8, 128),
         ),
-        [HBM] * 7,
+        [HBM] * 8,
         (HBM,) * 5,
-        scratch=[pltpu.SMEM(array.shape, jnp.int32) for array in (border_pick, recv_src, recv_pair, face_pick, face_pair)]
+        scratch=[pltpu.SMEM(array.shape, jnp.int32) for array in (local_pairs, border_pick, recv_src, recv_pair, face_pick, face_pair)]
         + [
             pltpu.VMEM((3, patches, 128), F32),
             pltpu.VMEM((patches, 128), F32),
             pltpu.VMEM((patches * 8, 128), F32),
+            pltpu.VMEM((pairs * 8, 128), F32),
             pltpu.VMEM((count, 4, 128), F32),
-            pltpu.VMEM((facing, 8, 128), F32),
-            pltpu.VMEM((facing, 8, 128), F32),
+            pltpu.VMEM((facing * 8, 128), F32),
+            pltpu.VMEM((facing * 8, 128), F32),
             pltpu.VMEM((border_pick.shape[1] * 8, 128), F32),
         ]
-        + [pltpu.SemaphoreType.DMA((n,)) for n in (5, 8, 4, 4)],
+        + [pltpu.SemaphoreType.DMA((n,)) for n in (6, 8, 5)],
         cost=(patches * 128 * 60, patches * 128 * 48, 0),
     )(
-        border_pick, recv_src, recv_pair, face_pick, face_pair,
+        local_pairs, border_pick, recv_src, recv_pair, face_pick, face_pair,
         jnp.transpose(verts, (1, 0, 2)), stiffness,
     )
 
@@ -455,7 +451,7 @@
         HBM,
         scratch=[
             pltpu.SMEM(local_pairs.shape, jnp.int32),
-            pltpu.VMEM((patches * 8, 128), F32),
+            pltpu.VMEM((pairs * 8, 128), F32),
             pltpu.VMEM((patches * 8, 128), F32),
             pltpu.VMEM((3, patches, 128), F32),
             pltpu.SemaphoreType.DMA((2,)),
@@ -463,7 +459,7 @@
         ]
         + tile_scratch(WIDTH),
         cost=(pairs * tile * 400, patches * 128 * 48, pairs * tile),
-    )(local_pairs, table)
+    )(local_pairs, near)
 
     back, brick_react = call(
         brick_kernel,
@@ -475,8 +471,8 @@
             pltpu.VMEM(arrived.shape, F32),
             pltpu.VMEM((count, 4, 128), F32),
             pltpu.VMEM((count * 8, 128), F32),
-            pltpu.SMEM((bricks, 128), F32),
-            pltpu.SemaphoreType.DMA((bricks + 2,)),
+            pltpu.SMEM((count, 128), F32),
+            pltpu.SemaphoreType.DMA((3,)),
         ]
         + tile_scratch(WIDTH),
         cost=(count * tile * 400, patches * 128 * 32, count * tile),
@@ -495,11 +491,10 @@
             pltpu.VMEM((count * 8, 128), F32),
             pltpu.VMEM((3, patches, 128), F32),
             pltpu.VMEM((patches * 8, 128), F32),
-            pltpu.VMEM((2, facing, 8, 128), F32),
-            pltpu.VMEM((2, facing, 8, 128), F32),
-            pltpu.SMEM((bricks, 128), F32),
-            pltpu.SemaphoreType.DMA((9,)),
-            pltpu.SemaphoreType.DMA((bricks,)),
+            pltpu.VMEM((2 * facing * 8, 128), F32),
+            pltpu.VMEM((2 * facing * 8, 128), F32),
+            pltpu.SMEM((count, 128), F32),
+            pltpu.SemaphoreType.DMA((10,)),
             pltpu.SemaphoreType.DMA((4,)),
         ]
         + tile_scratch(WIDTH),

time: 51.7 us -> 47.3 us (0.915)
  the two profiles are of different devices: /device:TPU:13 before, /device:TPU:11 now
where the time goes in v3:
time: 47.3 us; the launch traced here: 47 us
  Pallas kernels  33.3 us (70%)
  starting transfers between devices  13.7 us (29%)
    pallas_call x1, Pallas kernels, body(): call(local_kernel, shape(3, patches, 128), [HBM] * 2, HBM, scratch=[pltpu...  12.2 us
    pallas_call x1, Pallas kernels, body(): call(face_kernel, shape(3, patches, 128), [HBM] * 10, HBM, scratch=[pltpu...  8.33 us
    all_to_all x1, starting transfers between devices, body(): brick_push = lax.all_to_all(back, 'brick', 0, 0, tiled=True)  5.66 us
    all_to_all x1, starting transfers between devices, body(): arrived = lax.all_to_all(brick_msg, 'brick', 0, 0, tiled=True)  5.65 us
    pallas_call x1, Pallas kernels, body(): call(pack_kernel, (shape(pairs * 8, 128), shape(count, 4, 128), shape(fac...  4.87 us
    pallas_call x1, Pallas kernels, body(): call(brick_kernel, (shape(count, 4, 128), shape(count * 8, 128)), [HBM, H...  4.82 us
    pallas_call x1, Pallas kernels, body(): call(final_kernel, shape(3, patches, 128), [HBM, HBM, HBM], HBM, scratch=...  3.04 us
    ppermute x1, starting transfers between devices, body(): lax.ppermute(face_hi, 'slab', [(i, (i + 1) % layers) for i in range(layer...  2.11 us
  transfers between devices with their start and end apart: 4, of which 0 were waited for; matrix products, arithmetic and copies ran while one was open for 0% of the time, Pallas kernels for 54%

profile of v3, /device:TPU:11, one launch (start us, length us, event | category | flops | bytes accessed | tf_op | source)
XLA Modules:
  0.0 47.0 jit_solution(7569678185693141564)
XLA Ops:
  0.0 4.9 %shard_map.82 = (f32[2048,128]{1,0:T(8,128)}, f32[64,4,128]{2,1,0:T(4,128)}, f32[512,128]{1,0:T(8,128)}, f32[512,128]{1,0:T(8,128)}, f32[1024,128]{1,0:T(8,128)}) custom-call(s32[1,2,256]{2,1,0:T(2,128)} %local_any.3, s32[1,128]{1,0:T(1,128)} %border_any.3, s32[1,8,8]{2,1,0:T(8,128)} %src_any.1, s32[1,8,8]{2,1,0:T(8,128)} %pair_any.5, s32[1,2,64]{2,1,0:T(2,128)} %pick_any.3, ...), custom_call_target="tpu_custom_call" | custom-call | flops 7864320 | bytes 6291456 | tf_op jit(solution)/shard_map/pallas_call | solution.py:417
  4.9 5.6 %all-to-all-start = ((f32[64,4,128]{2,1,0:T(4,128)}), f32[64,4,128]{2,1,0:T(4,128)}, u32[]{:S(2)}, u32[]{:S(2)}) async-start(f32[64,4,128]{2,1,0:T(4,128)} %get-tuple-element.12), calls=%async_computation | async-start | bytes 262144 | tf_op jit(solution)/shard_map/all_to_all | solution.py:443
  10.5 0.3 collective-permute-start.1
  10.8 2.1 %collective-permute-start = (f32[512,128]{1,0:T(8,128)}, f32[512,128]{1,0:T(8,128)}, u32[]{:S(2)}, u32[]{:S(2)}) collective-permute-start(f32[512,128]{1,0:T(8,128)} %get-tuple-element.17.sent_hi), channel_id=1, source_target_pairs={{0,8},{8,16},{16,24},{24,0},{1,9},{9,17},{17,25},{25,1},{2,10},{10... | collective-permute-start | bytes 786440 | tf_op jit(solution)/shard_map/ppermute | solution.py:445
  12.9 12.2 %shard_map.83.after_any.planes_in = f32[3,1024,128]{2,1,0:T(8,128)} custom-call(s32[1,2,256]{2,1,0:T(2,128)} %local_any.3, f32[2048,128]{1,0:T(8,128)} %get-tuple-element.14.near_any), custom_call_target="tpu_custom_call" | custom-call | flops 1677721600 | bytes 6291456 | tf_op jit(solution)/shard_map/pallas_call | solution.py:447
  25.1 0.0 all-to-all-done.message_any.message
  25.1 4.8 %shard_map.84 = (f32[64,4,128]{2,1,0:T(4,128)}, f32[512,128]{1,0:T(8,128)}) custom-call(f32[1024,128]{1,0:T(8,128)} %get-tuple-element.13.border_any, f32[64,4,128]{2,1,0:T(4,128)} %all-to-all-done.message_any.message, f32[3,1024,128]{2,1,0:T(8,128)} %shard_map.83.after_any.planes_in), custom_call_target="tpu_custom_call" | custom-call | flops 419430400 | bytes 4194304 | tf_op jit(solution)/shard_map/pallas_call | solution.py:464
  29.9 5.7 %all-to-all-start.1 = ((f32[64,4,128]{2,1,0:T(4,128)}), f32[64,4,128]{2,1,0:T(4,128)}, u32[]{:S(2)}, u32[]{:S(2)}) async-start(f32[64,4,128]{2,1,0:T(4,128)} %get-tuple-element.18), calls=%async_computation.1 | async-start | bytes 262144 | tf_op jit(solution)/shard_map/all_to_all | solution.py:481
  35.6 0.0 collective-permute-done.1.got_hi
  35.6 0.0 collective-permute-done.got_lo
  35.6 8.3 %shard_map.85.planes_any = f32[3,1024,128]{2,1,0:T(8,128)} custom-call(s32[1,128]{1,0:T(1,128)} %border_any.3, s32[1,2,64]{2,1,0:T(2,128)} %pick_any.3, s32[1,2,64]{2,1,0:T(2,128)} %pair_any.4, f32[64,4,128]{2,1,0:T(4,128)} %all-to-all-done.message_any.message, f32[512,128]{1,0:T(8,128)} %get-tuple-element.15.react_any, ...), custom_call_target="tpu_custom_call" | custom-call | flops 1677721600 | bytes 8388608 | tf_op jit(solution)/shard_map/pallas_call | solution.py:482
  43.9 0.0 all-to-all-done.1.push_any
  43.9 3.0 %shard_map.86 = f32[3,1024,128]{2,1,0:T(8,128)} custom-call(s32[1,8,8]{2,1,0:T(8,128)} %pair_any.5, f32[3,1024,128]{2,1,0:T(8,128)} %shard_map.85.planes_any, f32[64,4,128]{2,1,0:T(4,128)} %all-to-all-done.1.push_any), custom_call_target="tpu_custom_call" | custom-call | flops 196608 | bytes 3145728 | tf_op jit(solution)/shard_map/pallas_call | solution.py:504
Async XLA Ops:
  4.9 20.2 %all-to-all-start = ((f32[64,4,128]{2,1,0:T(4,128)}), f32[64,4,128]{2,1,0:T(4,128)}, u32[]{:S(2)}, u32[]{:S(2)}) async-start(f32[64,4,128]{2,1,0:T(4,128)} %get-tuple-element.12), calls=%async_computation | async-start | bytes 262144 | tf_op jit(solution)/shard_map/all_to_all | solution.py:443
  10.5 25.1 %collective-permute-start.1 = (f32[512,128]{1,0:T(8,128)}, f32[512,128]{1,0:T(8,128)}, u32[]{:S(2)}, u32[]{:S(2)}) collective-permute-start(f32[512,128]{1,0:T(8,128)} %get-tuple-element.16.sent_lo), channel_id=1, source_target_pairs={{8,0},{16,8},{24,16},{0,24},{9,1},{17,9},{25,17},{1,25},{10,2},{18... | collective-permute-start | bytes 786440 | tf_op jit(solution)/shard_map/ppermute | solution.py:444
  10.8 24.8 %collective-permute-start = (f32[512,128]{1,0:T(8,128)}, f32[512,128]{1,0:T(8,128)}, u32[]{:S(2)}, u32[]{:S(2)}) collective-permute-start(f32[512,128]{1,0:T(8,128)} %get-tuple-element.17.sent_hi), channel_id=1, source_target_pairs={{0,8},{8,16},{16,24},{24,0},{1,9},{9,17},{17,25},{25,1},{2,10},{10... | collective-permute-start | bytes 786440 | tf_op jit(solution)/shard_map/ppermute | solution.py:445
  29.9 14.0 %all-to-all-start.1 = ((f32[64,4,128]{2,1,0:T(4,128)}), f32[64,4,128]{2,1,0:T(4,128)}, u32[]{:S(2)}, u32[]{:S(2)}) async-start(f32[64,4,128]{2,1,0:T(4,128)} %get-tuple-element.18), calls=%async_computation.1 | async-start | bytes 262144 | tf_op jit(solution)/shard_map/all_to_all | solution.py:481

commit v4 on v3

--- a/solution.py
+++ b/solution.py
@@ -76,7 +76,7 @@
     ]
 
 
-def run_tiles(start, stop, width, load, finish, scratch):
+def run_tiles(start, stop, width, load, finish, scratch, filled=None, beside=None):
     lefts, rights, thins, highs, lows, sums = scratch
     row = row_index()
 
@@ -111,7 +111,9 @@
     for q in range(width):
         energies(q)
 
-    sums[width:] = jnp.zeros((width, 2, 8, 128), F32)
+    sums[width : 2 * width] = jnp.zeros((width, 2, 8, 128), F32)
+    if filled is not None:
+        filled()
 
     @pl.loop(0, (stop - start) // (2 * width))
     def step(m):
@@ -120,6 +122,8 @@
             here, there = half * width, (1 - half) * width
             for q in range(width):
                 finish(jnp.maximum(base + here + q - width, start), sums[there + q, 0], sums[there + q, 1])
+                if beside is not None:
+                    beside(base + here + q)
                 sums[here + q, 0], sums[here + q, 1] = totals(here + q)
                 energies(there + q)
                 prepare(jnp.minimum(base + 2 * width + here + q, last), here + q)
@@ -137,7 +141,7 @@
 
 
 def width_for(couples):
-    return math.gcd(couples, 2 * WIDTH) // 2
+    return max(width for width in range(1, WIDTH + 1) if couples % (2 * width) == 0)
 
 
 def build_table(verts, stiffness, table, first, last):
@@ -159,6 +163,10 @@
         ref[pl.ds(pl.multiple_of(n * 64, 64), 64), :] = jnp.zeros((64, 128), F32)
 
 
+def slot_of(n, slots):
+    return n + jnp.where(n >= lax.axis_index("brick") * slots, slots, 0)
+
+
 def message_index(message, index, sem):
     return pltpu.make_async_copy(message.at[:, 3, :], index, sem)
 
@@ -178,11 +186,28 @@
     return [pltpu.make_async_copy(source, target, sem.at[first + n]) for n, (source, target) in enumerate(pairs)]
 
 
+def ask_kernel(src_any, pair_any, verts_any, brick_any, recv_src, recv_pair, verts, brick_msg, sem):
+    wait_all(start_all(copies_of(((src_any, recv_src), (pair_any, recv_pair), (verts_any, verts)), sem)))
+    bricks, slots = recv_pair.shape[1], recv_pair.shape[2]
+
+    @pl.loop(0, bricks, unroll=4)
+    def brick(s):
+        for k in range(slots):
+            target = recv_pair[0, s, k]
+            wanted = jnp.where(target >= 0, recv_src[0, s, k], -1).astype(F32)
+            place = pl.ds(jnp.maximum(target, 0), 1)
+            for c in range(3):
+                brick_msg[s * slots + k, c:c + 1] = verts[c, place, :] * ALPHA
+            brick_msg[s * slots + k, 3:4] = jnp.full((1, 128), wanted, F32)
+
+    wait_all(start_all(copies_of([(brick_msg, brick_any)], sem)))
+
+
 def pack_kernel(
-    local_any, border_any, src_any, pair_any, pick_any, facing_any, verts_any, stiffness_any,
-    near_any, brick_any, lo_any, hi_any, border_out,
-    local_pairs, border_pick, recv_src, recv_pair, face_pick, face_pair, verts, stiffness, table, near,
-    brick_msg, face_lo, face_hi, border, small_sem, large_sem, out_sem,
+    local_any, border_any, pick_any, facing_any, verts_any, stiffness_any,
+    near_any, lo_any, hi_any, border_out,
+    local_pairs, border_pick, face_pick, face_pair, verts, stiffness, table, near,
+    face_lo, face_hi, border, small_sem, large_sem, out_sem,
 ):
     patches = stiffness.shape[0]
     row = row_index()
@@ -194,8 +219,7 @@
         pieces = ((verts_any.at[:, here, :], verts.at[:, here, :]), (stiffness_any.at[here], stiffness.at[here]))
         large.append(start_all(copies_of(pieces, large_sem, 2 * part)))
     small = (
-        (local_any, local_pairs), (border_any, border_pick), (src_any, recv_src), (pair_any, recv_pair),
-        (pick_any, face_pick), (facing_any, face_pair),
+        (local_any, local_pairs), (border_any, border_pick), (pick_any, face_pick), (facing_any, face_pair),
     )
     small = start_all(copies_of(small, small_sem))
     sends = []
@@ -209,7 +233,7 @@
         own, far = entry_at(table, local_pairs[0, 0, n]), entry_at(table, local_pairs[0, 1, n])
         near[pl.ds(pl.multiple_of(n * 8, 8), 8), :] = jnp.where(row < 4, own, far)
 
-    sends += start_all(copies_of([(near, near_any)], out_sem, 4))
+    sends += start_all(copies_of([(near, near_any)], out_sem))
 
     @pl.loop(0, border.shape[0] // 8, unroll=16)
     def borders(n):
@@ -226,18 +250,6 @@
 
     sends += start_all(copies_of([(face_lo, lo_any), (face_hi, hi_any)], out_sem, 1))
 
-    bricks, slots = recv_pair.shape[1], recv_pair.shape[2]
-
-    @pl.loop(0, bricks, unroll=2)
-    def brick(s):
-        for k in range(slots):
-            target = recv_pair[0, s, k]
-            wanted = jnp.where(target >= 0, recv_src[0, s, k], -1).astype(F32)
-            entry = entry_at(table, jnp.maximum(target, 0))
-            brick_msg[s * slots + k] = jnp.where(row == 3, wanted, entry)[0:4]
-
-    sends += start_all(copies_of([(brick_msg, brick_any)], out_sem))
-
     wait_all(sends)
 
 
@@ -259,9 +271,14 @@
     wait_all(sends)
 
 
-def local_kernel(local_any, near_any, planes_out, local_pairs, near, force, planes, sem, plane_sem, *scratch):
+def local_kernel(local_any, near_any, after_any, planes_out, local_pairs, near, force, planes, sem, plane_sem, *scratch):
     row = row_index()
-    copies = start_all(copies_of([(local_any, local_pairs), (near_any, near)], sem))
+    pairs = local_pairs.shape[2]
+    width = width_for(pairs)
+    first = pl.ds(0, 2 * width * 8)
+    rest = pl.ds(2 * width * 8, (pairs - 2 * width) * 8)
+    copies = start_all(copies_of([(near_any.at[first], near.at[first])], sem))
+    others = start_all(copies_of([(local_any, local_pairs), (near_any.at[rest], near.at[rest])], sem, 1))
     clear_rows(force)
     wait_all(copies)
 
@@ -275,22 +292,24 @@
         add_at(force, local_pairs[0, 0, n], push_of(entry, push))
         add_at(force, local_pairs[0, 1, n], react_of(pltpu.roll(entry, 4, 0), react))
 
-    pairs = local_pairs.shape[2]
-    run_tiles(0, pairs, width_for(pairs), load, finish, scratch)
+    run_tiles(0, pairs, width, load, finish, scratch, lambda: wait_all(others))
     write_planes(force, planes, planes_out, plane_sem)
 
 
-def brick_kernel(border_any, message_any, after_any, back_any, react_any, border, message, back, react_out, index, sem, *scratch):
+def brick_kernel(border_any, message_any, back_any, react_any, border, message, back, react_out, index, sem, *scratch):
     row = row_index()
     count = message.shape[0]
     copies = [message_index(message_any, index, sem.at[2])]
     copies += copies_of(((border_any, border), (message_any, message)), sem)
     wait_all(start_all(copies))
 
+    slots = count // lax.axis_size("brick")
+
     def far_entry(n):
         return entry_at(border, jnp.maximum(index[n, 0].astype(jnp.int32), 0))
 
     def load(n):
+        n = slot_of(n, slots)
         x = jnp.concatenate([message[n], message[n]], axis=0)
         square = jnp.where(row < 3, x * x, 0.0)
         level = -0.5 * jnp.sum(square, axis=0, keepdims=True) + jnp.where(index[n, 0] >= 0.0, 0.0, OFF)
@@ -299,11 +318,13 @@
         return (far, own), (own, far)
 
     def finish(n, push, react):
+        n = slot_of(n, slots)
         back[n] = push_of(message[n], push[0:4])
         far = pltpu.roll(far_entry(n), 4, 0)
         react_out[pl.ds(pl.multiple_of(n * 8, 8), 8), :] = react_of(far, react)
 
-    run_tiles(0, count, width_for(count), load, finish, scratch)
+    couples = count - slots
+    run_tiles(0, couples, width_for(couples), load, finish, scratch)
     copies = [
         pltpu.make_async_copy(back, back_any, sem.at[0]),
         pltpu.make_async_copy(react_out, react_any, sem.at[1]),
@@ -315,35 +336,48 @@
 
 
 def face_kernel(
-    border_any, pick_any, pair_any, message, react_any, planes_in, sent_lo, sent_hi, got_lo, got_hi,
-    planes_out, border_pick, face_pick, face_pair, brick_react, planes, force, sent, got, index, sem, plane_sem,
+    border_any, pick_any, pair_any, asked_any, message, react_any, push_any, planes_in, sent_lo, sent_hi, got_lo, got_hi,
+    planes_out, border_pick, face_pick, face_pair, recv_pair, brick_react, brick_push, planes, force, sent, got, index, sem, plane_sem,
     *scratch,
 ):
     row = row_index()
     facing = face_pick.shape[2]
-    copies = [message_index(message, index, sem.at[9])]
+    copies = [message_index(message, index, sem.at[11])]
     for side, (mine, theirs) in enumerate(((sent_lo, got_lo), (sent_hi, got_hi))):
         here = pl.ds(side * facing * 8, facing * 8)
         copies.append(pltpu.make_async_copy(mine, sent.at[here], sem.at[side]))
         copies.append(pltpu.make_async_copy(theirs, got.at[here], sem.at[side + 2]))
     for n, (source, target) in enumerate(
-        ((border_any, border_pick), (pick_any, face_pick), (pair_any, face_pair), (react_any, brick_react))
+        (
+            (border_any, border_pick), (pick_any, face_pick), (pair_any, face_pair), (react_any, brick_react),
+            (asked_any, recv_pair), (push_any, brick_push),
+        )
     ):
         copies.append(pltpu.make_async_copy(source, target, sem.at[n + 4]))
-    before = pltpu.make_async_copy(planes_in, planes, sem.at[8])
+    before = pltpu.make_async_copy(planes_in, planes, sem.at[10])
     for copy in copies + [before]:
         copy.start()
     clear_rows(force)
     for copy in copies:
         copy.wait()
 
-    @pl.loop(0, index.shape[0], unroll=8)
-    def add_bricks(n):
-        anchor = border_pick[0, jnp.maximum(index[n, 0].astype(jnp.int32), 0)]
-        add_at(force, anchor, entry_at(brick_react, n))
-
     layer = lax.axis_index("slab")
     has_low, has_high = layer > 0, layer < lax.axis_size("slab") - 1
+
+    start = jnp.where(has_low, 0, facing)
+    stop = jnp.where(has_high, 2 * facing, facing)
+    bricks, slots = recv_pair.shape[1], recv_pair.shape[2]
+
+    @pl.loop(0, bricks - 1, unroll=1)
+    def add_bricks(n):
+        s = n + jnp.where(n >= lax.axis_index("brick"), 1, 0)
+        for k in range(slots):
+            slot = s * slots + k
+            anchor = border_pick[0, jnp.maximum(index[slot, 0].astype(jnp.int32), 0)]
+            add_at(force, anchor, entry_at(brick_react, slot))
+            target = recv_pair[0, s, k]
+            push = jnp.concatenate([brick_push[slot], jnp.zeros((4, 128), F32)], axis=0)
+            add_at(force, jnp.maximum(target, 0), jnp.where(target >= 0, push, 0.0))
 
     def load(n):
         mine, theirs = entry_at(sent, n), entry_at(got, n)
@@ -357,33 +391,10 @@
         add_at(force, jnp.maximum(face_pair[0, side, k], 0), push_of(mine, push))
         add_at(force, face_pick[0, side, k], react_of(pltpu.roll(mine, 4, 0), react))
 
-    start = jnp.where(has_low, 0, facing)
-    stop = jnp.where(has_high, 2 * facing, facing)
     run_tiles(start, stop, width_for(facing), load, finish, scratch)
 
     before.wait()
     write_planes(force, planes, planes_out, plane_sem, before)
-
-
-def final_kernel(pair_any, planes_any, push_any, out_any, recv_pair, low, mid, high, brick_push, in_sem, out_sem):
-    planes = (low, mid, high)
-    small = start_all(copies_of(((push_any, brick_push), (pair_any, recv_pair)), in_sem, 3))
-    large = start_all(copies_of([(planes_any.at[c], plane) for c, plane in enumerate(planes)], in_sem))
-    bricks, slots = recv_pair.shape[1], recv_pair.shape[2]
-    wait_all(small)
-    sends = []
-    for c, plane in enumerate(planes):
-        large[c].wait()
-
-        @pl.loop(0, bricks)
-        def brick(s):
-            for k in range(slots):
-                target = recv_pair[0, s, k]
-                push = jnp.where(target >= 0, brick_push[s * slots + k, c:c + 1], 0.0)
-                plane[pl.ds(jnp.maximum(target, 0), 1), :] += push
-
-        sends += start_all(copies_of([(plane, out_any.at[c])], out_sem, c))
-    wait_all(sends)
 
 
 HBM = pl.BlockSpec(memory_space=pltpu.HBM)
@@ -414,57 +425,52 @@
     layers = lax.axis_size("slab")
     tile = 128 * 128
 
-    near, brick_msg, face_lo, face_hi, border = call(
+    points = jnp.transpose(verts, (1, 0, 2))
+    brick_msg = call(
+        ask_kernel,
+        shape(count, 4, 128),
+        [HBM] * 3,
+        HBM,
+        scratch=[
+            pltpu.SMEM(recv_src.shape, jnp.int32),
+            pltpu.SMEM(recv_pair.shape, jnp.int32),
+            pltpu.VMEM((3, patches, 128), F32),
+            pltpu.VMEM((count, 4, 128), F32),
+            pltpu.SemaphoreType.DMA((3,)),
+        ],
+        cost=(count * 512, patches * 128 * 12, 0),
+    )(recv_src, recv_pair, points)
+    arrived = lax.all_to_all(brick_msg, "brick", 0, 0, tiled=True)
+
+    near, face_lo, face_hi, border = call(
         pack_kernel,
         (
-            shape(pairs * 8, 128), shape(count, 4, 128), shape(facing * 8, 128), shape(facing * 8, 128),
+            shape(pairs * 8, 128), shape(facing * 8, 128), shape(facing * 8, 128),
             shape(border_pick.shape[1] * 8, 128),
         ),
-        [HBM] * 8,
-        (HBM,) * 5,
-        scratch=[pltpu.SMEM(array.shape, jnp.int32) for array in (local_pairs, border_pick, recv_src, recv_pair, face_pick, face_pair)]
+        [HBM] * 6,
+        (HBM,) * 4,
+        scratch=[pltpu.SMEM(array.shape, jnp.int32) for array in (local_pairs, border_pick, face_pick, face_pair)]
         + [
             pltpu.VMEM((3, patches, 128), F32),
             pltpu.VMEM((patches, 128), F32),
             pltpu.VMEM((patches * 8, 128), F32),
             pltpu.VMEM((pairs * 8, 128), F32),
-            pltpu.VMEM((count, 4, 128), F32),
             pltpu.VMEM((facing * 8, 128), F32),
             pltpu.VMEM((facing * 8, 128), F32),
             pltpu.VMEM((border_pick.shape[1] * 8, 128), F32),
         ]
-        + [pltpu.SemaphoreType.DMA((n,)) for n in (6, 8, 5)],
+        + [pltpu.SemaphoreType.DMA((n,)) for n in (4, 8, 4)],
         cost=(patches * 128 * 60, patches * 128 * 48, 0),
-    )(
-        local_pairs, border_pick, recv_src, recv_pair, face_pick, face_pair,
-        jnp.transpose(verts, (1, 0, 2)), stiffness,
-    )
-
-    arrived = lax.all_to_all(brick_msg, "brick", 0, 0, tiled=True)
+    )(local_pairs, border_pick, face_pick, face_pair, points, stiffness)
+
     got_hi = lax.ppermute(face_lo, "slab", [((i + 1) % layers, i) for i in range(layers)])
     got_lo = lax.ppermute(face_hi, "slab", [(i, (i + 1) % layers) for i in range(layers)])
-
-    planes = call(
-        local_kernel,
-        shape(3, patches, 128),
-        [HBM] * 2,
-        HBM,
-        scratch=[
-            pltpu.SMEM(local_pairs.shape, jnp.int32),
-            pltpu.VMEM((pairs * 8, 128), F32),
-            pltpu.VMEM((patches * 8, 128), F32),
-            pltpu.VMEM((3, patches, 128), F32),
-            pltpu.SemaphoreType.DMA((2,)),
-            pltpu.SemaphoreType.DMA((4,)),
-        ]
-        + tile_scratch(WIDTH),
-        cost=(pairs * tile * 400, patches * 128 * 48, pairs * tile),
-    )(local_pairs, near)
 
     back, brick_react = call(
         brick_kernel,
         (shape(count, 4, 128), shape(count * 8, 128)),
-        [HBM, HBM, HBM],
+        [HBM, HBM],
         (HBM, HBM),
         scratch=[
             pltpu.VMEM(border.shape, F32),
@@ -476,41 +482,52 @@
         ]
         + tile_scratch(WIDTH),
         cost=(count * tile * 400, patches * 128 * 32, count * tile),
-    )(border, arrived, planes)
+    )(border, arrived)
 
     brick_push = lax.all_to_all(back, "brick", 0, 0, tiled=True)
     planes = call(
+        local_kernel,
+        shape(3, patches, 128),
+        [HBM] * 3,
+        HBM,
+        scratch=[
+            pltpu.SMEM(local_pairs.shape, jnp.int32),
+            pltpu.VMEM((pairs * 8, 128), F32),
+            pltpu.VMEM((patches * 8, 128), F32),
+            pltpu.VMEM((3, patches, 128), F32),
+            pltpu.SemaphoreType.DMA((3,)),
+            pltpu.SemaphoreType.DMA((4,)),
+        ]
+        + tile_scratch(WIDTH),
+        cost=(pairs * tile * 400, patches * 128 * 48, pairs * tile),
+    )(local_pairs, near, back)
+
+    out = call(
         face_kernel,
         shape(3, patches, 128),
-        [HBM] * 10,
+        [HBM] * 12,
         HBM,
         scratch=[
             pltpu.SMEM(border_pick.shape, jnp.int32),
             pltpu.SMEM(face_pick.shape, jnp.int32),
             pltpu.SMEM(face_pair.shape, jnp.int32),
+            pltpu.SMEM(recv_pair.shape, jnp.int32),
             pltpu.VMEM((count * 8, 128), F32),
+            pltpu.VMEM((count, 4, 128), F32),
             pltpu.VMEM((3, patches, 128), F32),
             pltpu.VMEM((patches * 8, 128), F32),
             pltpu.VMEM((2 * facing * 8, 128), F32),
             pltpu.VMEM((2 * facing * 8, 128), F32),
             pltpu.SMEM((count, 128), F32),
-            pltpu.SemaphoreType.DMA((10,)),
+            pltpu.SemaphoreType.DMA((12,)),
             pltpu.SemaphoreType.DMA((4,)),
         ]
         + tile_scratch(WIDTH),
         cost=(4 * facing * tile * 400, patches * 128 * 64, 4 * facing * tile),
-    )(border_pick, face_pick, face_pair, arrived, brick_react, planes, face_lo, face_hi, got_lo, got_hi)
-
-    out = call(
-        final_kernel,
-        shape(3, patches, 128),
-        [HBM, HBM, HBM],
-        HBM,
-        scratch=[pltpu.SMEM(recv_pair.shape, jnp.int32)]
-        + [pltpu.VMEM((patches, 128), F32)] * 3
-        + [pltpu.VMEM((count, 4, 128), F32), pltpu.SemaphoreType.DMA((5,)), pltpu.SemaphoreType.DMA((3,))],
-        cost=(count * 128 * 24, patches * 128 * 24, 0),
-    )(recv_pair, planes, brick_push)
+    )(
+        border_pick, face_pick, face_pair, recv_pair, arrived, brick_react, brick_push, planes,
+        face_lo, face_hi, got_lo, got_hi,
+    )
     return jnp.transpose(out, (1, 0, 2))
 
 

time: 47.3 us -> 46.6 us (0.985)
  Pallas kernels: 33.3 us -> 32.3 us
    pallas_call x4, Pallas kernels: 28.4 us -> 27.4 us  [the longest x1 11.8 us: body(): call(local_kernel, shape(3, patches, 128), [HBM] * 3, HBM, scratch=[pltpu...]
  transfers between devices with their start and end apart: 4 -> 4, of which waited for: 0 -> 0; matrix products, arithmetic and copies ran while one was open for 0% -> 0% of each run, Pallas kernels for 54% -> 46%
where the time goes in v4:
time: 46.6 us; the launch traced here: 46.1 us
  Pallas kernels  32.3 us (69%)
  starting transfers between devices  13.7 us (29%)
    pallas_call x1, Pallas kernels, body(): call(local_kernel, shape(3, patches, 128), [HBM] * 3, HBM, scratch=[pltpu...  11.8 us
    pallas_call x1, Pallas kernels, body(): call(face_kernel, shape(3, patches, 128), [HBM] * 12, HBM, scratch=[pltpu...  8.61 us
    all_to_all x1, starting transfers between devices, body(): brick_push = lax.all_to_all(back, 'brick', 0, 0, tiled=True)  5.68 us
    all_to_all x1, starting transfers between devices, body(): arrived = lax.all_to_all(brick_msg, 'brick', 0, 0, tiled=True)  5.65 us
    pallas_call x1, Pallas kernels, body(): call(brick_kernel, (shape(count, 4, 128), shape(count * 8, 128)), [HBM, H...  4.87 us
    pallas_call x1, Pallas kernels, body(): call(pack_kernel, (shape(pairs * 8, 128), shape(facing * 8, 128), shape(f...  4.77 us
    pallas_call x1, Pallas kernels, body(): call(ask_kernel, shape(count, 4, 128), [HBM] * 3, HBM, scratch=[pltpu.SME...  2.28 us
    ppermute x1, starting transfers between devices, body(): lax.ppermute(face_hi, 'slab', [(i, (i + 1) % layers) for i in range(layer...  2.11 us
  transfers between devices with their start and end apart: 4, of which 0 were waited for; matrix products, arithmetic and copies ran while one was open for 0% of the time, Pallas kernels for 46%

profile of v4, /device:TPU:11, one launch (start us, length us, event | category | flops | bytes accessed | tf_op | source)
XLA Modules:
  0.0 46.1 jit_solution(18207459454831786507)
XLA Ops:
  0.0 2.3 %shard_map.82 = f32[64,4,128]{2,1,0:T(4,128)} custom-call(s32[1,8,8]{2,1,0:T(8,128)} %src_any.1, s32[1,8,8]{2,1,0:T(8,128)} %asked_any.1, f32[3,1024,128]{2,1,0:T(8,128)} %bitcast.2), custom_call_target="tpu_custom_call" | custom-call | flops 32768 | bytes 1572864 | tf_op jit(solution)/shard_map/pallas_call | solution.py:429
  2.3 5.6 %all-to-all-start = ((f32[64,4,128]{2,1,0:T(4,128)}), f32[64,4,128]{2,1,0:T(4,128)}, u32[]{:S(2)}, u32[]{:S(2)}) async-start(f32[64,4,128]{2,1,0:T(4,128)} %shard_map.82), calls=%async_computation | async-start | bytes 262144 | tf_op jit(solution)/shard_map/all_to_all | solution.py:443
  7.9 4.8 %shard_map.83 = (f32[2048,128]{1,0:T(8,128)}, f32[512,128]{1,0:T(8,128)}, f32[512,128]{1,0:T(8,128)}, f32[1024,128]{1,0:T(8,128)}) custom-call(s32[1,2,256]{2,1,0:T(2,128)} %local_any.3, s32[1,128]{1,0:T(1,128)} %border_any.3, s32[1,2,64]{2,1,0:T(2,128)} %pick_any.3, s32[1,2,64]{2,1,0:T(2,128)} %pair_any.3, f32[3,1024,128]{2,1,0:T(8,128)} %bitcast.3, ...), custom_call_target="tpu_custom_call" | custom-call | flops 7864320 | bytes 6291456 | tf_op jit(solution)/shard_map/pallas_call | solution.py:445
  12.7 0.3 collective-permute-start.1
  13.0 2.1 %collective-permute-start = (f32[512,128]{1,0:T(8,128)}, f32[512,128]{1,0:T(8,128)}, u32[]{:S(2)}, u32[]{:S(2)}) collective-permute-start(f32[512,128]{1,0:T(8,128)} %get-tuple-element.16.sent_hi), channel_id=1, source_target_pairs={{0,8},{8,16},{16,24},{24,0},{1,9},{9,17},{17,25},{25,1},{2,10},{10... | collective-permute-start | bytes 786440 | tf_op jit(solution)/shard_map/ppermute | solution.py:468
  15.1 0.0 all-to-all-done.message_any.message
  15.1 4.9 %shard_map.84 = (f32[64,4,128]{2,1,0:T(4,128)}, f32[512,128]{1,0:T(8,128)}) custom-call(f32[1024,128]{1,0:T(8,128)} %get-tuple-element.11.border_any, f32[64,4,128]{2,1,0:T(4,128)} %all-to-all-done.message_any.message), custom_call_target="tpu_custom_call" | custom-call | flops 419430400 | bytes 4194304 | tf_op jit(solution)/shard_map/pallas_call | solution.py:470
  20.0 5.7 %all-to-all-start.1 = ((f32[64,4,128]{2,1,0:T(4,128)}), f32[64,4,128]{2,1,0:T(4,128)}, u32[]{:S(2)}, u32[]{:S(2)}) async-start(f32[64,4,128]{2,1,0:T(4,128)} %get-tuple-element.13.after_any), calls=%async_computation.1 | async-start | bytes 262144 | tf_op jit(solution)/shard_map/all_to_all | solution.py:487
  25.7 11.8 %shard_map.85.planes_in = f32[3,1024,128]{2,1,0:T(8,128)} custom-call(s32[1,2,256]{2,1,0:T(2,128)} %local_any.3, f32[2048,128]{1,0:T(8,128)} %get-tuple-element.14.near_any, f32[64,4,128]{2,1,0:T(4,128)} %get-tuple-element.13.after_any), custom_call_target="tpu_custom_call" | custom-call | flops 1677721600 | bytes 6291456 | tf_op jit(solution)/shard_map/pallas_call | solution.py:488
  37.5 0.0 collective-permute-done.1.got_hi
  37.5 0.0 collective-permute-done.got_lo
  37.5 0.0 all-to-all-done.1.push_any
  37.5 8.6 %shard_map.86 = f32[3,1024,128]{2,1,0:T(8,128)} custom-call(s32[1,128]{1,0:T(1,128)} %border_any.3, s32[1,2,64]{2,1,0:T(2,128)} %pick_any.3, s32[1,2,64]{2,1,0:T(2,128)} %pair_any.3, s32[1,8,8]{2,1,0:T(8,128)} %asked_any.1, f32[64,4,128]{2,1,0:T(4,128)} %all-to-all-done.message_any.message, f32[512,128]{1,0:T(8,128)} %get-tuple-element.12.react_any, ...), custom_call_target="tpu_custom_call" | custom-call | flops 1677721600 | bytes 8388608 | tf_op jit(solution)/shard_map/pallas_call | solution.py:505
Async XLA Ops:
  2.3 12.8 %all-to-all-start = ((f32[64,4,128]{2,1,0:T(4,128)}), f32[64,4,128]{2,1,0:T(4,128)}, u32[]{:S(2)}, u32[]{:S(2)}) async-start(f32[64,4,128]{2,1,0:T(4,128)} %shard_map.82), calls=%async_computation | async-start | bytes 262144 | tf_op jit(solution)/shard_map/all_to_all | solution.py:443
  12.7 24.8 %collective-permute-start.1 = (f32[512,128]{1,0:T(8,128)}, f32[512,128]{1,0:T(8,128)}, u32[]{:S(2)}, u32[]{:S(2)}) collective-permute-start(f32[512,128]{1,0:T(8,128)} %get-tuple-element.15.sent_lo), channel_id=1, source_target_pairs={{8,0},{16,8},{24,16},{0,24},{9,1},{17,9},{25,17},{1,25},{10,2},{18... | collective-permute-start | bytes 786440 | tf_op jit(solution)/shard_map/ppermute | solution.py:467
  13.0 24.5 %collective-permute-start = (f32[512,128]{1,0:T(8,128)}, f32[512,128]{1,0:T(8,128)}, u32[]{:S(2)}, u32[]{:S(2)}) collective-permute-start(f32[512,128]{1,0:T(8,128)} %get-tuple-element.16.sent_hi), channel_id=1, source_target_pairs={{0,8},{8,16},{16,24},{24,0},{1,9},{9,17},{17,25},{25,1},{2,10},{10... | collective-permute-start | bytes 786440 | tf_op jit(solution)/shard_map/ppermute | solution.py:468
  20.0 17.5 %all-to-all-start.1 = ((f32[64,4,128]{2,1,0:T(4,128)}), f32[64,4,128]{2,1,0:T(4,128)}, u32[]{:S(2)}, u32[]{:S(2)}) async-start(f32[64,4,128]{2,1,0:T(4,128)} %get-tuple-element.13.after_any), calls=%async_computation.1 | async-start | bytes 262144 | tf_op jit(solution)/shard_map/all_to_all | solution.py:487

commit v5 on v4

--- a/solution.py
+++ b/solution.py
@@ -206,7 +206,7 @@
 def pack_kernel(
     local_any, border_any, pick_any, facing_any, verts_any, stiffness_any,
     near_any, lo_any, hi_any, border_out,
-    local_pairs, border_pick, face_pick, face_pair, verts, stiffness, table, near,
+    own_side, far_side, border_pick, face_pick, face_pair, verts, stiffness, table, near,
     face_lo, face_hi, border, small_sem, large_sem, out_sem,
 ):
     patches = stiffness.shape[0]
@@ -219,7 +219,8 @@
         pieces = ((verts_any.at[:, here, :], verts.at[:, here, :]), (stiffness_any.at[here], stiffness.at[here]))
         large.append(start_all(copies_of(pieces, large_sem, 2 * part)))
     small = (
-        (local_any, local_pairs), (border_any, border_pick), (pick_any, face_pick), (facing_any, face_pair),
+        (local_any.at[0, 0], own_side), (local_any.at[0, 1], far_side),
+        (border_any.at[0], border_pick), (pick_any, face_pick), (facing_any, face_pair),
     )
     small = start_all(copies_of(small, small_sem))
     sends = []
@@ -230,14 +231,14 @@
 
     @pl.loop(0, near.shape[0] // 8, unroll=16)
     def pairs(n):
-        own, far = entry_at(table, local_pairs[0, 0, n]), entry_at(table, local_pairs[0, 1, n])
+        own, far = entry_at(table, own_side[n]), entry_at(table, far_side[n])
         near[pl.ds(pl.multiple_of(n * 8, 8), 8), :] = jnp.where(row < 4, own, far)
 
     sends += start_all(copies_of([(near, near_any)], out_sem))
 
     @pl.loop(0, border.shape[0] // 8, unroll=16)
     def borders(n):
-        border[pl.ds(pl.multiple_of(n * 8, 8), 8), :] = entry_at(table, border_pick[0, n])
+        border[pl.ds(pl.multiple_of(n * 8, 8), 8), :] = entry_at(table, border_pick[n])
 
     sends += start_all(copies_of([(border, border_out)], out_sem, 3))
     @pl.loop(0, face_lo.shape[0] // 8, unroll=8)
@@ -271,14 +272,17 @@
     wait_all(sends)
 
 
-def local_kernel(local_any, near_any, after_any, planes_out, local_pairs, near, force, planes, sem, plane_sem, *scratch):
+def local_kernel(
+    local_any, near_any, after_any, planes_out, own_side, far_side, near, force, planes, sem, plane_sem, *scratch,
+):
     row = row_index()
-    pairs = local_pairs.shape[2]
+    pairs = own_side.shape[0]
     width = width_for(pairs)
     first = pl.ds(0, 2 * width * 8)
     rest = pl.ds(2 * width * 8, (pairs - 2 * width) * 8)
     copies = start_all(copies_of([(near_any.at[first], near.at[first])], sem))
-    others = start_all(copies_of([(local_any, local_pairs), (near_any.at[rest], near.at[rest])], sem, 1))
+    pieces = ((local_any.at[0, 0], own_side), (local_any.at[0, 1], far_side), (near_any.at[rest], near.at[rest]))
+    others = start_all(copies_of(pieces, sem, 1))
     clear_rows(force)
     wait_all(copies)
 
@@ -289,8 +293,8 @@
 
     def finish(n, push, react):
         entry = entry_at(near, n)
-        add_at(force, local_pairs[0, 0, n], push_of(entry, push))
-        add_at(force, local_pairs[0, 1, n], react_of(pltpu.roll(entry, 4, 0), react))
+        add_at(force, own_side[n], push_of(entry, push))
+        add_at(force, far_side[n], react_of(pltpu.roll(entry, 4, 0), react))
 
     run_tiles(0, pairs, width, load, finish, scratch, lambda: wait_all(others))
     write_planes(force, planes, planes_out, plane_sem)
@@ -337,29 +341,34 @@
 
 def face_kernel(
     border_any, pick_any, pair_any, asked_any, message, react_any, push_any, planes_in, sent_lo, sent_hi, got_lo, got_hi,
-    planes_out, border_pick, face_pick, face_pair, recv_pair, brick_react, brick_push, planes, force, sent, got, index, sem, plane_sem,
+    planes_out, border_pick, face_pick, face_pair, recv_pair, brick_react, brick_push, planes, force, sent, got, index, sem, head_sem, plane_sem,
     *scratch,
 ):
     row = row_index()
     facing = face_pick.shape[2]
-    copies = [message_index(message, index, sem.at[11])]
+    width = width_for(facing)
+    first = 2 * width * 8
+    heads, copies = [], [message_index(message, index, sem.at[11])]
     for side, (mine, theirs) in enumerate(((sent_lo, got_lo), (sent_hi, got_hi))):
-        here = pl.ds(side * facing * 8, facing * 8)
-        copies.append(pltpu.make_async_copy(mine, sent.at[here], sem.at[side]))
-        copies.append(pltpu.make_async_copy(theirs, got.at[here], sem.at[side + 2]))
+        base = side * facing * 8
+        for n, (source, target) in enumerate(((mine, sent), (theirs, got))):
+            head, rest = pl.ds(base, first), pl.ds(base + first, facing * 8 - first)
+            heads.append(pltpu.make_async_copy(source.at[pl.ds(0, first)], target.at[head], head_sem.at[2 * side + n]))
+            copies.append(
+                pltpu.make_async_copy(source.at[pl.ds(first, facing * 8 - first)], target.at[rest], sem.at[2 * side + n])
+            )
     for n, (source, target) in enumerate(
         (
-            (border_any, border_pick), (pick_any, face_pick), (pair_any, face_pair), (react_any, brick_react),
+            (border_any.at[0], border_pick), (pick_any, face_pick), (pair_any, face_pair), (react_any, brick_react),
             (asked_any, recv_pair), (push_any, brick_push),
         )
     ):
         copies.append(pltpu.make_async_copy(source, target, sem.at[n + 4]))
     before = pltpu.make_async_copy(planes_in, planes, sem.at[10])
-    for copy in copies + [before]:
+    for copy in heads + copies + [before]:
         copy.start()
     clear_rows(force)
-    for copy in copies:
-        copy.wait()
+    wait_all(heads)
 
     layer = lax.axis_index("slab")
     has_low, has_high = layer > 0, layer < lax.axis_size("slab") - 1
@@ -368,16 +377,19 @@
     stop = jnp.where(has_high, 2 * facing, facing)
     bricks, slots = recv_pair.shape[1], recv_pair.shape[2]
 
-    @pl.loop(0, bricks - 1, unroll=1)
-    def add_bricks(n):
+    def add_brick(n):
         s = n + jnp.where(n >= lax.axis_index("brick"), 1, 0)
         for k in range(slots):
             slot = s * slots + k
-            anchor = border_pick[0, jnp.maximum(index[slot, 0].astype(jnp.int32), 0)]
+            anchor = border_pick[jnp.maximum(index[slot, 0].astype(jnp.int32), 0)]
             add_at(force, anchor, entry_at(brick_react, slot))
             target = recv_pair[0, s, k]
             push = jnp.concatenate([brick_push[slot], jnp.zeros((4, 128), F32)], axis=0)
             add_at(force, jnp.maximum(target, 0), jnp.where(target >= 0, push, 0.0))
+
+    def add_bricks():
+        wait_all(copies)
+        pl.loop(0, bricks - 1)(add_brick)
 
     def load(n):
         mine, theirs = entry_at(sent, n), entry_at(got, n)
@@ -391,7 +403,7 @@
         add_at(force, jnp.maximum(face_pair[0, side, k], 0), push_of(mine, push))
         add_at(force, face_pick[0, side, k], react_of(pltpu.roll(mine, 4, 0), react))
 
-    run_tiles(start, stop, width_for(facing), load, finish, scratch)
+    run_tiles(start, stop, width, load, finish, scratch, add_bricks)
 
     before.wait()
     write_planes(force, planes, planes_out, plane_sem, before)
@@ -450,7 +462,8 @@
         ),
         [HBM] * 6,
         (HBM,) * 4,
-        scratch=[pltpu.SMEM(array.shape, jnp.int32) for array in (local_pairs, border_pick, face_pick, face_pair)]
+        scratch=[pltpu.SMEM((pairs,), jnp.int32)] * 2
+        + [pltpu.SMEM(dims, jnp.int32) for dims in (border_pick.shape[1:], face_pick.shape, face_pair.shape)]
         + [
             pltpu.VMEM((3, patches, 128), F32),
             pltpu.VMEM((patches, 128), F32),
@@ -460,7 +473,7 @@
             pltpu.VMEM((facing * 8, 128), F32),
             pltpu.VMEM((border_pick.shape[1] * 8, 128), F32),
         ]
-        + [pltpu.SemaphoreType.DMA((n,)) for n in (4, 8, 4)],
+        + [pltpu.SemaphoreType.DMA((n,)) for n in (5, 8, 4)],
         cost=(patches * 128 * 60, patches * 128 * 48, 0),
     )(local_pairs, border_pick, face_pick, face_pair, points, stiffness)
 
@@ -491,11 +504,12 @@
         [HBM] * 3,
         HBM,
         scratch=[
-            pltpu.SMEM(local_pairs.shape, jnp.int32),
+            pltpu.SMEM((pairs,), jnp.int32),
+            pltpu.SMEM((pairs,), jnp.int32),
             pltpu.VMEM((pairs * 8, 128), F32),
             pltpu.VMEM((patches * 8, 128), F32),
             pltpu.VMEM((3, patches, 128), F32),
-            pltpu.SemaphoreType.DMA((3,)),
+            pltpu.SemaphoreType.DMA((4,)),
             pltpu.SemaphoreType.DMA((4,)),
         ]
         + tile_scratch(WIDTH),
@@ -508,7 +522,7 @@
         [HBM] * 12,
         HBM,
         scratch=[
-            pltpu.SMEM(border_pick.shape, jnp.int32),
+            pltpu.SMEM(border_pick.shape[1:], jnp.int32),
             pltpu.SMEM(face_pick.shape, jnp.int32),
             pltpu.SMEM(face_pair.shape, jnp.int32),
             pltpu.SMEM(recv_pair.shape, jnp.int32),
@@ -520,6 +534,7 @@
             pltpu.VMEM((2 * facing * 8, 128), F32),
             pltpu.SMEM((count, 128), F32),
             pltpu.SemaphoreType.DMA((12,)),
+            pltpu.SemaphoreType.DMA((4,)),
             pltpu.SemaphoreType.DMA((4,)),
         ]
         + tile_scratch(WIDTH),

time: 46.6 us -> 45.7 us (0.981)
  Pallas kernels: 32.3 us -> 31.5 us
where the time goes in v5:
time: 45.7 us; the launch traced here: 45.2 us
  Pallas kernels  31.5 us (69%)
  starting transfers between devices  13.7 us (30%)
    pallas_call x1, Pallas kernels, body(): call(local_kernel, shape(3, patches, 128), [HBM] * 3, HBM, scratch=[pltpu...  11.7 us
    pallas_call x1, Pallas kernels, body(): call(face_kernel, shape(3, patches, 128), [HBM] * 12, HBM, scratch=[pltpu...  8.17 us
    all_to_all x1, starting transfers between devices, body(): arrived = lax.all_to_all(brick_msg, 'brick', 0, 0, tiled=True)  5.65 us
    all_to_all x1, starting transfers between devices, body(): brick_push = lax.all_to_all(back, 'brick', 0, 0, tiled=True)  5.64 us
    pallas_call x1, Pallas kernels, body(): call(brick_kernel, (shape(count, 4, 128), shape(count * 8, 128)), [HBM, H...  4.88 us
    pallas_call x1, Pallas kernels, body(): call(pack_kernel, (shape(pairs * 8, 128), shape(facing * 8, 128), shape(f...  4.39 us
    pallas_call x1, Pallas kernels, body(): call(ask_kernel, shape(count, 4, 128), [HBM] * 3, HBM, scratch=[pltpu.SME...  2.28 us
    ppermute x1, starting transfers between devices, body(): lax.ppermute(face_hi, 'slab', [(i, (i + 1) % layers) for i in range(layer...  2.11 us
  transfers between devices with their start and end apart: 4, of which 0 were waited for; matrix products, arithmetic and copies ran while one was open for 0% of the time, Pallas kernels for 46%

profile of v5, /device:TPU:11, one launch (start us, length us, event | category | flops | bytes accessed | tf_op | source)
XLA Modules:
  0.0 45.2 jit_solution(18105522202930360055)
XLA Ops:
  0.0 2.3 %shard_map.82 = f32[64,4,128]{2,1,0:T(4,128)} custom-call(s32[1,8,8]{2,1,0:T(8,128)} %src_any.1, s32[1,8,8]{2,1,0:T(8,128)} %asked_any.1, f32[3,1024,128]{2,1,0:T(8,128)} %bitcast.2), custom_call_target="tpu_custom_call" | custom-call | flops 32768 | bytes 1572864 | tf_op jit(solution)/shard_map/pallas_call | solution.py:441
  2.3 5.6 %all-to-all-start = ((f32[64,4,128]{2,1,0:T(4,128)}), f32[64,4,128]{2,1,0:T(4,128)}, u32[]{:S(2)}, u32[]{:S(2)}) async-start(f32[64,4,128]{2,1,0:T(4,128)} %shard_map.82), calls=%async_computation | async-start | bytes 262144 | tf_op jit(solution)/shard_map/all_to_all | solution.py:455
  7.9 4.4 %shard_map.83 = (f32[2048,128]{1,0:T(8,128)}, f32[512,128]{1,0:T(8,128)}, f32[512,128]{1,0:T(8,128)}, f32[1024,128]{1,0:T(8,128)}) custom-call(s32[1,2,256]{2,1,0:T(2,128)} %local_any.3, s32[1,128]{1,0:T(1,128)} %border_any.3, s32[1,2,64]{2,1,0:T(2,128)} %pick_any.3, s32[1,2,64]{2,1,0:T(2,128)} %pair_any.3, f32[3,1024,128]{2,1,0:T(8,128)} %bitcast.3, ...), custom_call_target="tpu_custom_call" | custom-call | flops 7864320 | bytes 6291456 | tf_op jit(solution)/shard_map/pallas_call | solution.py:457
  12.3 0.3 collective-permute-start.1
  12.6 2.1 %collective-permute-start = (f32[512,128]{1,0:T(8,128)}, f32[512,128]{1,0:T(8,128)}, u32[]{:S(2)}, u32[]{:S(2)}) collective-permute-start(f32[512,128]{1,0:T(8,128)} %get-tuple-element.16.sent_hi), channel_id=1, source_target_pairs={{0,8},{8,16},{16,24},{24,0},{1,9},{9,17},{17,25},{25,1},{2,10},{10... | collective-permute-start | bytes 786440 | tf_op jit(solution)/shard_map/ppermute | solution.py:481
  14.7 0.0 all-to-all-done.message_any.message
  14.8 4.9 %shard_map.84 = (f32[64,4,128]{2,1,0:T(4,128)}, f32[512,128]{1,0:T(8,128)}) custom-call(f32[1024,128]{1,0:T(8,128)} %get-tuple-element.11.border_any, f32[64,4,128]{2,1,0:T(4,128)} %all-to-all-done.message_any.message), custom_call_target="tpu_custom_call" | custom-call | flops 419430400 | bytes 4194304 | tf_op jit(solution)/shard_map/pallas_call | solution.py:483
  19.6 5.6 %all-to-all-start.1 = ((f32[64,4,128]{2,1,0:T(4,128)}), f32[64,4,128]{2,1,0:T(4,128)}, u32[]{:S(2)}, u32[]{:S(2)}) async-start(f32[64,4,128]{2,1,0:T(4,128)} %get-tuple-element.13.after_any), calls=%async_computation.1 | async-start | bytes 262144 | tf_op jit(solution)/shard_map/all_to_all | solution.py:500
  25.3 11.7 %shard_map.85.planes_in = f32[3,1024,128]{2,1,0:T(8,128)} custom-call(s32[1,2,256]{2,1,0:T(2,128)} %local_any.3, f32[2048,128]{1,0:T(8,128)} %get-tuple-element.14.near_any, f32[64,4,128]{2,1,0:T(4,128)} %get-tuple-element.13.after_any), custom_call_target="tpu_custom_call" | custom-call | flops 1677721600 | bytes 6291456 | tf_op jit(solution)/shard_map/pallas_call | solution.py:501
  37.0 0.0 collective-permute-done.1.got_hi
  37.0 0.0 collective-permute-done.got_lo
  37.0 0.0 all-to-all-done.1.push_any
  37.1 8.2 %shard_map.86 = f32[3,1024,128]{2,1,0:T(8,128)} custom-call(s32[1,128]{1,0:T(1,128)} %border_any.3, s32[1,2,64]{2,1,0:T(2,128)} %pick_any.3, s32[1,2,64]{2,1,0:T(2,128)} %pair_any.3, s32[1,8,8]{2,1,0:T(8,128)} %asked_any.1, f32[64,4,128]{2,1,0:T(4,128)} %all-to-all-done.message_any.message, f32[512,128]{1,0:T(8,128)} %get-tuple-element.12.react_any, ...), custom_call_target="tpu_custom_call" | custom-call | flops 1677721600 | bytes 8388608 | tf_op jit(solution)/shard_map/pallas_call | solution.py:519
Async XLA Ops:
  2.3 12.5 %all-to-all-start = ((f32[64,4,128]{2,1,0:T(4,128)}), f32[64,4,128]{2,1,0:T(4,128)}, u32[]{:S(2)}, u32[]{:S(2)}) async-start(f32[64,4,128]{2,1,0:T(4,128)} %shard_map.82), calls=%async_computation | async-start | bytes 262144 | tf_op jit(solution)/shard_map/all_to_all | solution.py:455
  12.3 24.7 %collective-permute-start.1 = (f32[512,128]{1,0:T(8,128)}, f32[512,128]{1,0:T(8,128)}, u32[]{:S(2)}, u32[]{:S(2)}) collective-permute-start(f32[512,128]{1,0:T(8,128)} %get-tuple-element.15.sent_lo), channel_id=1, source_target_pairs={{8,0},{16,8},{24,16},{0,24},{9,1},{17,9},{25,17},{1,25},{10,2},{18... | collective-permute-start | bytes 786440 | tf_op jit(solution)/shard_map/ppermute | solution.py:480
  12.6 24.4 %collective-permute-start = (f32[512,128]{1,0:T(8,128)}, f32[512,128]{1,0:T(8,128)}, u32[]{:S(2)}, u32[]{:S(2)}) collective-permute-start(f32[512,128]{1,0:T(8,128)} %get-tuple-element.16.sent_hi), channel_id=1, source_target_pairs={{0,8},{8,16},{16,24},{24,0},{1,9},{9,17},{17,25},{25,1},{2,10},{10... | collective-permute-start | bytes 786440 | tf_op jit(solution)/shard_map/ppermute | solution.py:481
  19.6 17.4 %all-to-all-start.1 = ((f32[64,4,128]{2,1,0:T(4,128)}), f32[64,4,128]{2,1,0:T(4,128)}, u32[]{:S(2)}, u32[]{:S(2)}) async-start(f32[64,4,128]{2,1,0:T(4,128)} %get-tuple-element.13.after_any), calls=%async_computation.1 | async-start | bytes 262144 | tf_op jit(solution)/shard_map/all_to_all | solution.py:500

commit v6 on v5

--- a/solution.py
+++ b/solution.py
@@ -76,7 +76,7 @@
     ]
 
 
-def run_tiles(start, stop, width, load, finish, scratch, filled=None, beside=None):
+def run_tiles(start, stop, width, load, finish, scratch, filled=None, narrow=False):
     lefts, rights, thins, highs, lows, sums = scratch
     row = row_index()
 
@@ -88,8 +88,12 @@
         second = jnp.concatenate(empty + far_rows(far_across, row), axis=0)
         lefts[slot] = jnp.concatenate(left, axis=0).astype(BF16).T
         rights[slot] = jnp.concatenate([first, second], axis=1).astype(BF16)
-        thin = jnp.concatenate([far_down[0], far_down[1], own_down[0], own_down[1]], axis=0)
-        thins[slot] = thin.astype(BF16)
+        thin = [far_down[0], far_down[1], own_down[0], own_down[1]]
+        if narrow:
+            thin_far = jnp.where(row < 4, far_down[0], jnp.where(row < 7, far_down[1], 0.0))
+            thin_own = jnp.where(row >= 4, own_down[0], jnp.where(row < 3, own_down[1], 0.0))
+            thin = [thin_far, thin_own]
+        thins[slot, 0 : 8 * len(thin), :] = jnp.concatenate(thin, axis=0).astype(BF16)
 
     def energies(slot):
         energy = jnp.exp2(lax.dot_general(lefts[slot], rights[slot], MATMUL, preferred_element_type=F32))
@@ -99,8 +103,13 @@
 
     def totals(slot):
         tall = jnp.concatenate([highs[slot], lows[slot]], axis=0)
-        thin = jnp.concatenate([thins[slot], thins[slot]], axis=1)
+        thin = thins[slot, 0 : 16 if narrow else 32, :]
+        thin = jnp.concatenate([thin, thin], axis=1)
         result = lax.dot_general(thin, tall, MATMUL, preferred_element_type=F32)
+        if narrow:
+            push, react = result[0:8, 0:128], result[8:16, 128:256]
+            push, react = push + pltpu.roll(push, 4, 0), react + pltpu.roll(react, 4, 0)
+            return push, react
         push = result[0:8, 0:128] + result[8:16, 0:128]
         react = result[16:24, 128:256] + result[24:32, 128:256]
         return push, react
@@ -122,8 +131,6 @@
             here, there = half * width, (1 - half) * width
             for q in range(width):
                 finish(jnp.maximum(base + here + q - width, start), sums[there + q, 0], sums[there + q, 1])
-                if beside is not None:
-                    beside(base + here + q)
                 sums[here + q, 0], sums[here + q, 1] = totals(here + q)
                 energies(there + q)
                 prepare(jnp.minimum(base + 2 * width + here + q, last), here + q)
@@ -328,7 +335,7 @@
         react_out[pl.ds(pl.multiple_of(n * 8, 8), 8), :] = react_of(far, react)
 
     couples = count - slots
-    run_tiles(0, couples, width_for(couples), load, finish, scratch)
+    run_tiles(0, couples, width_for(couples), load, finish, scratch, narrow=True)
     copies = [
         pltpu.make_async_copy(back, back_any, sem.at[0]),
         pltpu.make_async_copy(react_out, react_any, sem.at[1]),

time: 45.7 us -> 45.5 us (level)
  no operation moved by 1% of the time
where the time goes in v6:
time: 45.5 us; the launch traced here: 45 us
  Pallas kernels  31.2 us (69%)
  starting transfers between devices  13.7 us (30%)
    pallas_call x1, Pallas kernels, body(): call(local_kernel, shape(3, patches, 128), [HBM] * 3, HBM, scratch=[pltpu...  11.7 us
    pallas_call x1, Pallas kernels, body(): call(face_kernel, shape(3, patches, 128), [HBM] * 12, HBM, scratch=[pltpu...  8.19 us
    all_to_all x1, starting transfers between devices, body(): brick_push = lax.all_to_all(back, 'brick', 0, 0, tiled=True)  5.68 us
    all_to_all x1, starting transfers between devices, body(): arrived = lax.all_to_all(brick_msg, 'brick', 0, 0, tiled=True)  5.65 us
    pallas_call x1, Pallas kernels, body(): call(brick_kernel, (shape(count, 4, 128), shape(count * 8, 128)), [HBM, H...  4.65 us
    pallas_call x1, Pallas kernels, body(): call(pack_kernel, (shape(pairs * 8, 128), shape(facing * 8, 128), shape(f...  4.39 us
    pallas_call x1, Pallas kernels, body(): call(ask_kernel, shape(count, 4, 128), [HBM] * 3, HBM, scratch=[pltpu.SME...  2.28 us
    ppermute x1, starting transfers between devices, body(): lax.ppermute(face_hi, 'slab', [(i, (i + 1) % layers) for i in range(layer...  2.11 us
  transfers between devices with their start and end apart: 4, of which 0 were waited for; matrix products, arithmetic and copies ran while one was open for 0% of the time, Pallas kernels for 46%

profile of v6, /device:TPU:11, one launch (start us, length us, event | category | flops | bytes accessed | tf_op | source)
XLA Modules:
  0.0 45.0 jit_solution(13538458505327457616)
XLA Ops:
  0.0 2.3 %shard_map.82 = f32[64,4,128]{2,1,0:T(4,128)} custom-call(s32[1,8,8]{2,1,0:T(8,128)} %src_any.1, s32[1,8,8]{2,1,0:T(8,128)} %asked_any.1, f32[3,1024,128]{2,1,0:T(8,128)} %bitcast.2), custom_call_target="tpu_custom_call" | custom-call | flops 32768 | bytes 1572864 | tf_op jit(solution)/shard_map/pallas_call | solution.py:448
  2.3 5.6 %all-to-all-start = ((f32[64,4,128]{2,1,0:T(4,128)}), f32[64,4,128]{2,1,0:T(4,128)}, u32[]{:S(2)}, u32[]{:S(2)}) async-start(f32[64,4,128]{2,1,0:T(4,128)} %shard_map.82), calls=%async_computation | async-start | bytes 262144 | tf_op jit(solution)/shard_map/all_to_all | solution.py:462
  7.9 4.4 %shard_map.83 = (f32[2048,128]{1,0:T(8,128)}, f32[512,128]{1,0:T(8,128)}, f32[512,128]{1,0:T(8,128)}, f32[1024,128]{1,0:T(8,128)}) custom-call(s32[1,2,256]{2,1,0:T(2,128)} %local_any.3, s32[1,128]{1,0:T(1,128)} %border_any.3, s32[1,2,64]{2,1,0:T(2,128)} %pick_any.3, s32[1,2,64]{2,1,0:T(2,128)} %pair_any.3, f32[3,1024,128]{2,1,0:T(8,128)} %bitcast.3, ...), custom_call_target="tpu_custom_call" | custom-call | flops 7864320 | bytes 6291456 | tf_op jit(solution)/shard_map/pallas_call | solution.py:464
  12.3 0.3 collective-permute-start.1
  12.6 2.1 %collective-permute-start = (f32[512,128]{1,0:T(8,128)}, f32[512,128]{1,0:T(8,128)}, u32[]{:S(2)}, u32[]{:S(2)}) collective-permute-start(f32[512,128]{1,0:T(8,128)} %get-tuple-element.16.sent_hi), channel_id=1, source_target_pairs={{0,8},{8,16},{16,24},{24,0},{1,9},{9,17},{17,25},{25,1},{2,10},{10... | collective-permute-start | bytes 786440 | tf_op jit(solution)/shard_map/ppermute | solution.py:488
  14.7 0.0 all-to-all-done.message_any.message
  14.8 4.6 %shard_map.84 = (f32[64,4,128]{2,1,0:T(4,128)}, f32[512,128]{1,0:T(8,128)}) custom-call(f32[1024,128]{1,0:T(8,128)} %get-tuple-element.11.border_any, f32[64,4,128]{2,1,0:T(4,128)} %all-to-all-done.message_any.message), custom_call_target="tpu_custom_call" | custom-call | flops 419430400 | bytes 4194304 | tf_op jit(solution)/shard_map/pallas_call | solution.py:490
  19.4 5.7 %all-to-all-start.1 = ((f32[64,4,128]{2,1,0:T(4,128)}), f32[64,4,128]{2,1,0:T(4,128)}, u32[]{:S(2)}, u32[]{:S(2)}) async-start(f32[64,4,128]{2,1,0:T(4,128)} %get-tuple-element.13.after_any), calls=%async_computation.1 | async-start | bytes 262144 | tf_op jit(solution)/shard_map/all_to_all | solution.py:507
  25.1 11.7 %shard_map.85.planes_in = f32[3,1024,128]{2,1,0:T(8,128)} custom-call(s32[1,2,256]{2,1,0:T(2,128)} %local_any.3, f32[2048,128]{1,0:T(8,128)} %get-tuple-element.14.near_any, f32[64,4,128]{2,1,0:T(4,128)} %get-tuple-element.13.after_any), custom_call_target="tpu_custom_call" | custom-call | flops 1677721600 | bytes 6291456 | tf_op jit(solution)/shard_map/pallas_call | solution.py:508
  36.8 0.0 collective-permute-done.1.got_hi
  36.8 0.0 collective-permute-done.got_lo
  36.8 0.0 all-to-all-done.1.push_any
  36.9 8.2 %shard_map.86 = f32[3,1024,128]{2,1,0:T(8,128)} custom-call(s32[1,128]{1,0:T(1,128)} %border_any.3, s32[1,2,64]{2,1,0:T(2,128)} %pick_any.3, s32[1,2,64]{2,1,0:T(2,128)} %pair_any.3, s32[1,8,8]{2,1,0:T(8,128)} %asked_any.1, f32[64,4,128]{2,1,0:T(4,128)} %all-to-all-done.message_any.message, f32[512,128]{1,0:T(8,128)} %get-tuple-element.12.react_any, ...), custom_call_target="tpu_custom_call" | custom-call | flops 1677721600 | bytes 8388608 | tf_op jit(solution)/shard_map/pallas_call | solution.py:526
Async XLA Ops:
  2.3 12.5 %all-to-all-start = ((f32[64,4,128]{2,1,0:T(4,128)}), f32[64,4,128]{2,1,0:T(4,128)}, u32[]{:S(2)}, u32[]{:S(2)}) async-start(f32[64,4,128]{2,1,0:T(4,128)} %shard_map.82), calls=%async_computation | async-start | bytes 262144 | tf_op jit(solution)/shard_map/all_to_all | solution.py:462
  12.3 24.5 %collective-permute-start.1 = (f32[512,128]{1,0:T(8,128)}, f32[512,128]{1,0:T(8,128)}, u32[]{:S(2)}, u32[]{:S(2)}) collective-permute-start(f32[512,128]{1,0:T(8,128)} %get-tuple-element.15.sent_lo), channel_id=1, source_target_pairs={{8,0},{16,8},{24,16},{0,24},{9,1},{17,9},{25,17},{1,25},{10,2},{18... | collective-permute-start | bytes 786440 | tf_op jit(solution)/shard_map/ppermute | solution.py:487
  12.6 24.2 %collective-permute-start = (f32[512,128]{1,0:T(8,128)}, f32[512,128]{1,0:T(8,128)}, u32[]{:S(2)}, u32[]{:S(2)}) collective-permute-start(f32[512,128]{1,0:T(8,128)} %get-tuple-element.16.sent_hi), channel_id=1, source_target_pairs={{0,8},{8,16},{16,24},{24,0},{1,9},{9,17},{17,25},{25,1},{2,10},{10... | collective-permute-start | bytes 786440 | tf_op jit(solution)/shard_map/ppermute | solution.py:488
  19.4 17.4 %all-to-all-start.1 = ((f32[64,4,128]{2,1,0:T(4,128)}), f32[64,4,128]{2,1,0:T(4,128)}, u32[]{:S(2)}, u32[]{:S(2)}) async-start(f32[64,4,128]{2,1,0:T(4,128)} %get-tuple-element.13.after_any), calls=%async_computation.1 | async-start | bytes 262144 | tf_op jit(solution)/shard_map/all_to_all | solution.py:507

commit v7 on v6

--- a/solution.py
+++ b/solution.py
@@ -267,7 +267,7 @@
     sends = []
     for part in range(parts):
 
-        @pl.loop(part * rows // 8, (part + 1) * rows // 8, unroll=32)
+        @pl.loop(part * rows // 8, (part + 1) * rows // 8, unroll=16)
         def unpack(n):
             here = pl.ds(pl.multiple_of(n * 8, 8), 8)
             for c in range(3):

time: 45.5 us -> 45.4 us (level)
  no operation moved by 1% of the time
where the time goes in v7:
time: 45.4 us; the launch traced here: 45 us
  Pallas kernels  31.2 us (69%)
  starting transfers between devices  13.7 us (30%)
    pallas_call x1, Pallas kernels, body(): call(local_kernel, shape(3, patches, 128), [HBM] * 3, HBM, scratch=[pltpu...  11.7 us
    pallas_call x1, Pallas kernels, body(): call(face_kernel, shape(3, patches, 128), [HBM] * 12, HBM, scratch=[pltpu...  8.19 us
    all_to_all x1, starting transfers between devices, body(): brick_push = lax.all_to_all(back, 'brick', 0, 0, tiled=True)  5.67 us
    all_to_all x1, starting transfers between devices, body(): arrived = lax.all_to_all(brick_msg, 'brick', 0, 0, tiled=True)  5.65 us
    pallas_call x1, Pallas kernels, body(): call(brick_kernel, (shape(count, 4, 128), shape(count * 8, 128)), [HBM, H...  4.65 us
    pallas_call x1, Pallas kernels, body(): call(pack_kernel, (shape(pairs * 8, 128), shape(facing * 8, 128), shape(f...  4.39 us
    pallas_call x1, Pallas kernels, body(): call(ask_kernel, shape(count, 4, 128), [HBM] * 3, HBM, scratch=[pltpu.SME...  2.28 us
    ppermute x1, starting transfers between devices, body(): lax.ppermute(face_hi, 'slab', [(i, (i + 1) % layers) for i in range(layer...  2.11 us
  transfers between devices with their start and end apart: 4, of which 0 were waited for; matrix products, arithmetic and copies ran while one was open for 0% of the time, Pallas kernels for 46%

profile of v7, /device:TPU:11, one launch (start us, length us, event | category | flops | bytes accessed | tf_op | source)
XLA Modules:
  0.0 45.0 jit_solution(10143769441275351633)
XLA Ops:
  0.0 2.3 %shard_map.82 = f32[64,4,128]{2,1,0:T(4,128)} custom-call(s32[1,8,8]{2,1,0:T(8,128)} %src_any.1, s32[1,8,8]{2,1,0:T(8,128)} %asked_any.1, f32[3,1024,128]{2,1,0:T(8,128)} %bitcast.2), custom_call_target="tpu_custom_call" | custom-call | flops 32768 | bytes 1572864 | tf_op jit(solution)/shard_map/pallas_call | solution.py:448
  2.3 5.6 %all-to-all-start = ((f32[64,4,128]{2,1,0:T(4,128)}), f32[64,4,128]{2,1,0:T(4,128)}, u32[]{:S(2)}, u32[]{:S(2)}) async-start(f32[64,4,128]{2,1,0:T(4,128)} %shard_map.82), calls=%async_computation | async-start | bytes 262144 | tf_op jit(solution)/shard_map/all_to_all | solution.py:462
  7.9 4.4 %shard_map.83 = (f32[2048,128]{1,0:T(8,128)}, f32[512,128]{1,0:T(8,128)}, f32[512,128]{1,0:T(8,128)}, f32[1024,128]{1,0:T(8,128)}) custom-call(s32[1,2,256]{2,1,0:T(2,128)} %local_any.3, s32[1,128]{1,0:T(1,128)} %border_any.3, s32[1,2,64]{2,1,0:T(2,128)} %pick_any.3, s32[1,2,64]{2,1,0:T(2,128)} %pair_any.3, f32[3,1024,128]{2,1,0:T(8,128)} %bitcast.3, ...), custom_call_target="tpu_custom_call" | custom-call | flops 7864320 | bytes 6291456 | tf_op jit(solution)/shard_map/pallas_call | solution.py:464
  12.3 0.3 collective-permute-start.1
  12.6 2.1 %collective-permute-start = (f32[512,128]{1,0:T(8,128)}, f32[512,128]{1,0:T(8,128)}, u32[]{:S(2)}, u32[]{:S(2)}) collective-permute-start(f32[512,128]{1,0:T(8,128)} %get-tuple-element.16.sent_hi), channel_id=1, source_target_pairs={{0,8},{8,16},{16,24},{24,0},{1,9},{9,17},{17,25},{25,1},{2,10},{10... | collective-permute-start | bytes 786440 | tf_op jit(solution)/shard_map/ppermute | solution.py:488
  14.7 0.0 all-to-all-done.message_any.message
  14.8 4.6 %shard_map.84 = (f32[64,4,128]{2,1,0:T(4,128)}, f32[512,128]{1,0:T(8,128)}) custom-call(f32[1024,128]{1,0:T(8,128)} %get-tuple-element.11.border_any, f32[64,4,128]{2,1,0:T(4,128)} %all-to-all-done.message_any.message), custom_call_target="tpu_custom_call" | custom-call | flops 419430400 | bytes 4194304 | tf_op jit(solution)/shard_map/pallas_call | solution.py:490
  19.4 5.7 %all-to-all-start.1 = ((f32[64,4,128]{2,1,0:T(4,128)}), f32[64,4,128]{2,1,0:T(4,128)}, u32[]{:S(2)}, u32[]{:S(2)}) async-start(f32[64,4,128]{2,1,0:T(4,128)} %get-tuple-element.13.after_any), calls=%async_computation.1 | async-start | bytes 262144 | tf_op jit(solution)/shard_map/all_to_all | solution.py:507
  25.1 11.7 %shard_map.85.planes_in = f32[3,1024,128]{2,1,0:T(8,128)} custom-call(s32[1,2,256]{2,1,0:T(2,128)} %local_any.3, f32[2048,128]{1,0:T(8,128)} %get-tuple-element.14.near_any, f32[64,4,128]{2,1,0:T(4,128)} %get-tuple-element.13.after_any), custom_call_target="tpu_custom_call" | custom-call | flops 1677721600 | bytes 6291456 | tf_op jit(solution)/shard_map/pallas_call | solution.py:508
  36.8 0.0 collective-permute-done.1.got_hi
  36.8 0.0 collective-permute-done.got_lo
  36.8 0.0 all-to-all-done.1.push_any
  36.8 8.2 %shard_map.86 = f32[3,1024,128]{2,1,0:T(8,128)} custom-call(s32[1,128]{1,0:T(1,128)} %border_any.3, s32[1,2,64]{2,1,0:T(2,128)} %pick_any.3, s32[1,2,64]{2,1,0:T(2,128)} %pair_any.3, s32[1,8,8]{2,1,0:T(8,128)} %asked_any.1, f32[64,4,128]{2,1,0:T(4,128)} %all-to-all-done.message_any.message, f32[512,128]{1,0:T(8,128)} %get-tuple-element.12.react_any, ...), custom_call_target="tpu_custom_call" | custom-call | flops 1677721600 | bytes 8388608 | tf_op jit(solution)/shard_map/pallas_call | solution.py:526
Async XLA Ops:
  2.3 12.5 %all-to-all-start = ((f32[64,4,128]{2,1,0:T(4,128)}), f32[64,4,128]{2,1,0:T(4,128)}, u32[]{:S(2)}, u32[]{:S(2)}) async-start(f32[64,4,128]{2,1,0:T(4,128)} %shard_map.82), calls=%async_computation | async-start | bytes 262144 | tf_op jit(solution)/shard_map/all_to_all | solution.py:462
  12.3 24.5 %collective-permute-start.1 = (f32[512,128]{1,0:T(8,128)}, f32[512,128]{1,0:T(8,128)}, u32[]{:S(2)}, u32[]{:S(2)}) collective-permute-start(f32[512,128]{1,0:T(8,128)} %get-tuple-element.15.sent_lo), channel_id=1, source_target_pairs={{8,0},{16,8},{24,16},{0,24},{9,1},{17,9},{25,17},{1,25},{10,2},{18... | collective-permute-start | bytes 786440 | tf_op jit(solution)/shard_map/ppermute | solution.py:487
  12.6 24.2 %collective-permute-start = (f32[512,128]{1,0:T(8,128)}, f32[512,128]{1,0:T(8,128)}, u32[]{:S(2)}, u32[]{:S(2)}) collective-permute-start(f32[512,128]{1,0:T(8,128)} %get-tuple-element.16.sent_hi), channel_id=1, source_target_pairs={{0,8},{8,16},{16,24},{24,0},{1,9},{9,17},{17,25},{25,1},{2,10},{10... | collective-permute-start | bytes 786440 | tf_op jit(solution)/shard_map/ppermute | solution.py:488
  19.4 17.4 %all-to-all-start.1 = ((f32[64,4,128]{2,1,0:T(4,128)}), f32[64,4,128]{2,1,0:T(4,128)}, u32[]{:S(2)}, u32[]{:S(2)}) async-start(f32[64,4,128]{2,1,0:T(4,128)} %get-tuple-element.13.after_any), calls=%async_computation.1 | async-start | bytes 262144 | tf_op jit(solution)/shard_map/all_to_all | solution.py:507
